TPU v7x, 32 devices: a whole 2x2x4 slice. The times are simulated.
32 devices in a mesh: freq: 8 (over z, y), chan: 2 (over x), expert: 2 (over core).
Axes of the slice: x: 2, y: 2, z: 4, core: 2. Of those that a mesh axis runs over, the one named last changes fastest.
Arguments:
- spectra: bfloat16 [2048, 1024], P('freq', ('chan', 'expert')), may hold values from -6 to 6
- spectral_filter: bfloat16 [2, 256, 8, 1024], P(None, None, 'freq', ('chan', 'expert')), may hold values from -5 to 5
- norm_gain: float32 [1024], replicated, may hold values from 0.1 to 1.9
- mlp_gate: bfloat16 [1024, 2048], P(None, ('chan', 'expert')), may hold values from -0.1875 to 0.1875
- mlp_up: bfloat16 [1024, 2048], P(None, ('chan', 'expert')), may hold values from -0.1875 to 0.1875
- mlp_down: bfloat16 [2048, 1024], P(('chan', 'expert')), may hold values from -0.125 to 0.125
- expert_gain: float32 [1024], replicated, may hold values from 0.1 to 1.9
- expert_gate: bfloat16 [8, 1024, 4096], P('freq', None, ('chan', 'expert')), may hold values from -0.1875 to 0.1875
- expert_up: bfloat16 [8, 1024, 4096], P('freq', None, ('chan', 'expert')), may hold values from -0.1875 to 0.1875
- expert_down: bfloat16 [8, 4096, 1024], P('freq', ('chan', 'expert')), may hold values from -0.09375 to 0.09375
- routes: int32 [2048, 2], P('freq'), may hold values from 0 to 7, all different within a row; in each aligned block of 256 rows (0 to 255, 256 to 511, ...) at most 128 rows name the same one
- combine: int32 [2048, 2], P('freq'), may hold values from 1 to 8
Outputs:
- layer_out: bfloat16 [2048, 1024], P('freq', ('chan', 'expert'))
Inputs may be any that keep to these rules, and one draw needn't show every extreme that they name: `routes`: in each aligned block of 256 rows (the rows of one device) no expert is named by more than 128 rows, a bound that some block reaches; the two experts of a row differ.
All inputs are finite; a program needn't handle non-finite values.
Results may differ from a plain program's by a relative error of at most 0.015.
Values may be sent and summed in bfloat16 or wider, within the bound.
A program may use at most 64 MiB of HBM per device.

v0:
```python
import math

import jax
import jax.numpy as jnp
from jax import lax
from jax.sharding import PartitionSpec as P

HIGH = lax.Precision.HIGHEST
EPS = 1e-06


def tables(height, breadth, modulus, col_start):
    left = lax.broadcasted_iota(jnp.int32, (height, breadth), 0)
    right = lax.broadcasted_iota(jnp.int32, (height, breadth), 1) + col_start
    angle = (left * right % modulus).astype(jnp.float32) * (2.0 * math.pi / modulus)
    return (jnp.cos(angle), jnp.sin(angle))


def precise(left, right):
    return jnp.dot(left, right, precision=HIGH, preferred_element_type=jnp.float32)


def matmul(left, right):
    return jnp.dot(left, right, preferred_element_type=jnp.float32)


def rms_rows(values, gain_vec):
    values = values.astype(jnp.float32)
    inverse_rms = lax.rsqrt(jnp.mean(values * values, axis=-1, keepdims=True) + EPS)
    return (values * inverse_rms * gain_vec).astype(jnp.bfloat16)


def gated(normed, gate_w, up_w):
    return (jax.nn.silu(matmul(normed, gate_w)) * matmul(normed, up_w)).astype(jnp.bfloat16)


def across_slabs(values):
    return lax.all_to_all(
        values.astype(jnp.bfloat16), "freq", split_axis=0, concat_axis=0, tiled=True
    ).astype(values.dtype)


def spectral_mix(signal, filter_pair):
    slabs = lax.axis_size("freq")
    length = signal.shape[0]
    channels = signal.shape[1]
    block_rows = length // slabs
    length_all = length * slabs
    my_slab = lax.axis_index("freq")
    cos_slab, sin_slab = tables(slabs, slabs, slabs, 0)
    cos_long, sin_long = tables(length, length, length, 0)
    gathered = across_slabs(signal).reshape(slabs, block_rows * channels)
    first_re = precise(cos_slab, gathered).reshape(slabs, block_rows, channels)
    first_im = -precise(sin_slab, gathered).reshape(slabs, block_rows, channels)
    twist_cos, twist_sin = tables(slabs, block_rows, length_all, my_slab * block_rows)
    twist_cos = twist_cos[:, :, None]
    twist_sin = twist_sin[:, :, None]
    turned_re = first_re * twist_cos + first_im * twist_sin
    turned_im = first_im * twist_cos - first_re * twist_sin
    packed = jnp.stack([turned_re, turned_im], axis=2).reshape(length, 2, channels)
    columns = across_slabs(packed)
    col_re = columns[:, 0]
    col_im = columns[:, 1]
    freq_re = precise(cos_long, col_re) + precise(sin_long, col_im)
    freq_im = precise(cos_long, col_im) - precise(sin_long, col_re)
    coef_re = filter_pair[0, :, 0].astype(jnp.float32)
    coef_im = filter_pair[1, :, 0].astype(jnp.float32)
    shaped_re = coef_re * freq_re - coef_im * freq_im
    shaped_im = coef_re * freq_im + coef_im * freq_re
    back_re = precise(cos_long, shaped_re) - precise(sin_long, shaped_im)
    back_im = precise(cos_long, shaped_im) + precise(sin_long, shaped_re)
    undo_cos, undo_sin = tables(length, 1, length_all, my_slab)
    spun_re = back_re * undo_cos - back_im * undo_sin
    spun_im = back_im * undo_cos + back_re * undo_sin
    packed_back = jnp.stack([spun_re, spun_im], axis=1)
    rows_back = across_slabs(packed_back).reshape(slabs, block_rows, 2, channels)
    real_rows = rows_back[:, :, 0].reshape(slabs, block_rows * channels)
    imag_rows = rows_back[:, :, 1].reshape(slabs, block_rows * channels)
    spatial = precise(cos_slab, real_rows) - precise(sin_slab, imag_rows)
    spatial = spatial.reshape(length, channels)
    return across_slabs(spatial) / length_all


def body(
    spectra,
    spectral_filter,
    norm_gain,
    mlp_gate,
    mlp_up,
    mlp_down,
    expert_gain,
    expert_gate,
    expert_up,
    expert_down,
    routes,
    combine,
):
    signal = spectra.astype(jnp.float32)
    mixed_sum = signal + spectral_mix(signal, spectral_filter)
    full_rows = lax.all_gather(
        mixed_sum.astype(jnp.bfloat16), ("chan", "expert"), axis=1, tiled=True
    )
    hidden = gated(rms_rows(full_rows, norm_gain), mlp_gate, mlp_up)
    encoded = mixed_sum + lax.psum_scatter(
        matmul(hidden, mlp_down).astype(jnp.bfloat16),
        ("chan", "expert"),
        scatter_dimension=1,
        tiled=True,
    ).astype(jnp.float32)
    encoded_half = encoded.astype(jnp.bfloat16)
    slabs = lax.axis_size("freq")
    length = spectra.shape[0]
    capacity = min(length, 4 * length // slabs)
    slots_all = slabs * capacity
    picks = routes.reshape(-1)
    onehot = (picks[:, None] == lax.broadcasted_iota(jnp.int32, (1, slabs), 1)).astype(jnp.int32)
    earlier = jnp.cumsum(onehot, axis=0) - onehot
    position = jnp.sum(earlier * onehot, axis=1)
    slot_ids = picks * capacity + position
    placed = lax.broadcasted_iota(jnp.int32, (slots_all, 1), 0) == slot_ids[None, :]
    placed = placed.reshape(slots_all, length, 2)
    send_table = jnp.any(placed, axis=2).astype(jnp.bfloat16)
    shares = combine.astype(jnp.float32) / 8.0
    merge_table = jnp.sum(jnp.where(placed, shares[None], 0.0), axis=2).astype(jnp.bfloat16)
    whole_rows = lax.all_gather(encoded_half, ("chan", "expert"), axis=1, tiled=True)
    outgoing = matmul(send_table, whole_rows).astype(jnp.bfloat16)
    arrived = lax.all_to_all(outgoing, "freq", split_axis=0, concat_axis=0, tiled=True)
    expert_in = rms_rows(arrived, expert_gain)
    expert_hidden = gated(expert_in, expert_gate[0], expert_up[0])
    partial_out = matmul(expert_hidden, expert_down[0])
    expert_out = lax.psum_scatter(
        partial_out.astype(jnp.bfloat16), ("chan", "expert"), scatter_dimension=1, tiled=True
    )
    returned = lax.all_to_all(expert_out, "freq", split_axis=0, concat_axis=0, tiled=True)
    routed_sum = lax.dot_general(
        merge_table, returned, (((0,), (0,)), ((), ())), preferred_element_type=jnp.float32
    )
    return (encoded + routed_sum).astype(jnp.bfloat16)


def solution(mesh):
    placed = (
        P("freq", ("chan", "expert")),
        P(None, None, "freq", ("chan", "expert")),
        P(),
        P(None, ("chan", "expert")),
        P(None, ("chan", "expert")),
        P(("chan", "expert"), None),
        P(),
        P("freq", None, ("chan", "expert")),
        P("freq", None, ("chan", "expert")),
        P("freq", ("chan", "expert"), None),
        P("freq", None),
        P("freq", None),
    )
    return jax.shard_map(
        body, mesh=mesh, in_specs=placed, out_specs=P("freq", ("chan", "expert")), check_vma=False
    )
```

profile of v0, /device:TPU:0, one launch (start us, length us, event | category | flops | bytes accessed | tf_op | source)
XLA Modules:
  0.0 236.5 jit_solution(17324238418321908441)
XLA Ops:
  6.5 7.4 %all-to-all-start = ((bf16[8,32,256]{2,1,0:T(8,128)(2,1)}), bf16[8,32,256]{2,1,0:T(8,128)(2,1)S(1)}, u32[]{:S(2)}, u32[]{:S(2)}) async-start(bf16[8,32,256]{2,1,0:T(8,128)(2,1)} %bitcast.107), calls=%async_computation | async-start | bytes 262144 | tf_op jit(solution)/shard_map/all_to_all | solution.py:38
  14.1 7.2 %all-to-all-done = bf16[8,32,256]{2,1,0:T(8,128)(2,1)S(1)} async-done(((bf16[8,32,256]{2,1,0:T(8,128)(2,1)}), bf16[8,32,256]{2,1,0:T(8,128)(2,1)S(1)}, u32[]{:S(2)}, u32[]{:S(2)}) %all-to-all-start) | async-done | bytes 131104 | tf_op jit(solution)/shard_map/all_to_all | solution.py:38
  22.1 1.0 copy.66
  23.0 3.4 %all-to-all-start.1 = ((bf16[256,2,256]{2,1,0:T(2,128)(2,1)}), bf16[256,2,256]{2,1,0:T(2,128)(2,1)S(1)}, u32[]{:S(2)}, u32[]{:S(2)}) async-start(bf16[256,2,256]{2,1,0:T(2,128)(2,1)} %copy.66), calls=%async_computation.1 | async-start | bytes 524288 | tf_op jit(solution)/shard_map/all_to_all | solution.py:38
  26.5 8.1 %all-to-all-done.1 = bf16[256,2,256]{2,1,0:T(2,128)(2,1)S(1)} async-done(((bf16[256,2,256]{2,1,0:T(2,128)(2,1)}), bf16[256,2,256]{2,1,0:T(2,128)(2,1)S(1)}, u32[]{:S(2)}, u32[]{:S(2)}) %all-to-all-start.1) | async-done | bytes 262176 | tf_op jit(solution)/shard_map/all_to_all | solution.py:38
  35.0 1.2 fusion.50
  36.2 1.2 fusion.48
  37.4 1.2 convolution_add_fusion.1
  38.7 1.2 convolution_subtract_fusion.2
  39.9 1.4 fusion.44
  41.3 1.4 fusion.46
  42.8 1.4 convolution_add_fusion
  44.2 1.4 fusion.40
  45.9 11.2 %all_to_all.46 = bf16[256,2,256]{2,1,0:T(2,128)(2,1)S(1)} all-to-all(bf16[256,2,256]{2,1,0:T(2,128)(2,1)S(1)} %copy.69), channel_id=1, replica_groups=mesh['freq'=8,'chan'=2,'expert'=2] {'freq'}, dimensions={0} | all-to-all | bytes 524288 | tf_op jit(solution)/shard_map/all_to_all | solution.py:38
  57.1 1.1 slice_reduce_fusion
  59.1 10.0 %all_to_all.47 = bf16[8,32,256]{2,1,0:T(8,128)(2,1)S(1)} all-to-all(bf16[8,32,256]{2,1,0:T(8,128)(2,1)S(1)} %copy.72), channel_id=1, replica_groups=mesh['freq'=8,'chan'=2,'expert'=2] {'freq'}, dimensions={0} | all-to-all | bytes 262144 | tf_op jit(solution)/shard_map/all_to_all | solution.py:38
  69.2 7.1 %all_gather.6 = bf16[256,1024]{1,0:T(8,128)(2,1)S(1)} all-gather(bf16[256,256]{1,0:T(8,128)(2,1)S(1)} %get-tuple-element.7), channel_id=1, replica_groups=mesh['freq'=8,'chan'=2,'expert'=2] {'chan','expert'}, dimensions={1}, use_global_device_ids=true | all-gather | bytes 655360 | tf_op jit(solution)/shard_map/all_gather | solution.py:100
  77.0 3.2 %convolution_convert_fusion.1 = bf16[256,1024]{1,0:T(8,128)(2,1)} fusion(bf16[512,1024]{1,0:T(8,128)(2,1)} %param.17, bf16[1024,512]{1,0:T(8,128)(2,1)} %param.16, f32[256,512]{1,0:T(8,128)S(1)} %fusion.38, bf16[256,1024]{1,0:T(8,128)(2,1)S(1)} %all_gather.6, f32[1024]{0:T(1024)S(1)} %copy-done.9, f32[256]{0:T(256)S(1)} %add_rsqrt_fusion.1), kind=kOutput, calls=%fused_computation.20 | convolution fusion | flops 538968064 | bytes 3675136 | tf_op jit(solution)/shard_map/dot_general | solution.py:24
  80.8 1.1 reduce-window.6
  82.9 16.4 %reduce-scatter.3.cloned.1.call-done = bf16[256,256]{1,0:T(8,128)(2,1)} async-done(((bf16[256,1024]{1,0:T(8,128)(2,1)}), bf16[256,256]{1,0:T(8,128)(2,1)}) %reduce-scatter.3.cloned.1.call-update) | async-done | bytes 131088 | tf_op jit(solution)/shard_map/reduce_scatter | solution.py:104
  99.3 0.9 fusion.35
  100.2 6.8 %all_gather.7 = bf16[256,1024]{1,0:T(8,128)(2,1)S(1)} all-gather(bf16[256,256]{1,0:T(8,128)(2,1)S(1)} %fusion.35), channel_id=1, replica_groups=mesh['freq'=8,'chan'=2,'expert'=2] {'chan','expert'}, dimensions={1}, use_global_device_ids=true | all-gather | bytes 655360 | tf_op jit(solution)/shard_map/all_gather | solution.py:125
  107.0 0.7 convolution_convert_fusion
  107.7 54.0 %all_to_all.48 = bf16[8,128,1024]{2,1,0:T(8,128)(2,1)S(1)} all-to-all(bf16[8,128,1024]{2,1,0:T(8,128)(2,1)S(1)} %bitcast.98), channel_id=1, replica_groups=mesh['freq'=8,'chan'=2,'expert'=2] {'freq'}, dimensions={0} | all-to-all | bytes 4194304 | tf_op jit(solution)/shard_map/all_to_all | solution.py:127
  162.5 0.5 fusion.3
  163.0 1.3 copy-done.1
  164.3 4.3 %fusion.7 = f32[1024,1024]{1,0:T(8,128)} fusion(bf16[1024,1024]{1,0:T(8,128)(2,1)S(1)} %bitcast.101, bf16[1,1024,1024]{2,1,0:T(8,128)(2,1)S(1)} %copy-done), kind=kOutput, calls=%fused_computation.11 | convolution fusion | flops 2147483648 | bytes 8388608 | tf_op jit(solution)/shard_map/dot_general | solution.py:24
  168.6 9.9 %fusion.10 = bf16[1024,1024]{1,0:T(8,128)(2,1)} fusion(bf16[1,1024,1024]{2,1,0:T(8,128)(2,1)} %param.21, f32[1024,1024]{1,0:T(8,128)} %fusion.7, bf16[1024,1024]{1,0:T(8,128)(2,1)} %bitcast.102, bf16[1,1024,1024]{2,1,0:T(8,128)(2,1)} %param.20), kind=kOutput, calls=%fused_computation.16 | convolution fusion | flops 4302307328 | bytes 12582912 | tf_op jit(solution)/shard_map/dot_general | solution.py:24
  178.6 30.1 %reduce-scatter.5.cloned.1.call-done = bf16[1024,256]{1,0:T(8,128)(2,1)} async-done(((bf16[1024,1024]{1,0:T(8,128)(2,1)}), bf16[1024,256]{1,0:T(8,128)(2,1)}) %reduce-scatter.5.cloned.1.call-update) | async-done | bytes 524304 | tf_op jit(solution)/shard_map/reduce_scatter | solution.py:131
  208.6 5.5 %all-to-all-start.5 = ((bf16[8,128,256]{2,1,0:T(8,128)(2,1)}), bf16[8,128,256]{2,1,0:T(8,128)(2,1)S(1)}, u32[]{:S(2)}, u32[]{:S(2)}) async-start(bf16[8,128,256]{2,1,0:T(8,128)(2,1)} %bitcast.106), calls=%async_computation.7 | async-start | bytes 1048576 | tf_op jit(solution)/shard_map/all_to_all | solution.py:134
  214.6 14.0 %all-to-all-done.5 = bf16[8,128,256]{2,1,0:T(8,128)(2,1)S(1)} async-done(((bf16[8,128,256]{2,1,0:T(8,128)(2,1)}), bf16[8,128,256]{2,1,0:T(8,128)(2,1)S(1)}, u32[]{:S(2)}, u32[]{:S(2)}) %all-to-all-start.5) | async-done | bytes 524320 | tf_op jit(solution)/shard_map/all_to_all | solution.py:134
  228.7 1.0 fusion.16
  (60 shorter events, 5.8 us)
Async XLA Ops:
  6.5 157.8 %copy-start = (bf16[1,1024,1024]{2,1,0:T(8,128)(2,1)S(1)}, bf16[1,1024,1024]{2,1,0:T(8,128)(2,1)}, u32[]{:S(2)}) copy-start(bf16[1,1024,1024]{2,1,0:T(8,128)(2,1)} %param.19) | copy-start | bytes 6291460
  6.5 14.8 %all-to-all-start = ((bf16[8,32,256]{2,1,0:T(8,128)(2,1)}), bf16[8,32,256]{2,1,0:T(8,128)(2,1)S(1)}, u32[]{:S(2)}, u32[]{:S(2)}) async-start(bf16[8,32,256]{2,1,0:T(8,128)(2,1)} %bitcast.107), calls=%async_computation | async-start | bytes 262144 | tf_op jit(solution)/shard_map/all_to_all | solution.py:38
  23.0 11.6 %all-to-all-start.1 = ((bf16[256,2,256]{2,1,0:T(2,128)(2,1)}), bf16[256,2,256]{2,1,0:T(2,128)(2,1)S(1)}, u32[]{:S(2)}, u32[]{:S(2)}) async-start(bf16[256,2,256]{2,1,0:T(2,128)(2,1)} %copy.66), calls=%async_computation.1 | async-start | bytes 524288 | tf_op jit(solution)/shard_map/all_to_all | solution.py:38
  26.4 72.9 %reduce-scatter.3.cloned.1.call-start = ((), (), s32[]{:S(2)}) async-start(), calls=%async_computation.8 | async-start | bytes 655360 | tf_op jit(solution)/shard_map/reduce_scatter | solution.py:104
  36.2 3.7 %copy-start.8 = (bf16[2,256,1,256]{3,1,2,0:T(8,128)(2,1)S(1)}, bf16[2,256,1,256]{3,1,2,0:T(8,128)(2,1)}, u32[]{:S(2)}) copy-start(bf16[2,256,1,256]{3,1,2,0:T(8,128)(2,1)} %param.13) | copy-start | bytes 786436
  45.7 23.5 %copy-start.3 = (bf16[256,256]{1,0:T(8,128)(2,1)S(1)}, bf16[256,256]{1,0:T(8,128)(2,1)}, u32[]{:S(2)}) copy-start(bf16[256,256]{1,0:T(8,128)(2,1)} %param.12) | copy-start | bytes 393220
  58.3 18.2 %copy-start.7 = (bf16[1024,512]{1,0:T(8,128)(2,1)S(1)}, bf16[1024,512]{1,0:T(8,128)(2,1)}, u32[]{:S(2)}) copy-start(bf16[1024,512]{1,0:T(8,128)(2,1)} %param.15) | copy-start | bytes 3145732
  58.3 18.2 %copy-start.9 = (f32[1024]{0:T(1024)S(1)}, f32[1024]{0:T(1024)}, u32[]{:S(2)}) copy-start(f32[1024]{0:T(1024)} %param.14) | copy-start | bytes 12292
  77.0 3.3 %copy-start.4 = (s32[256,2]{0,1:T(2,128)S(1)}, s32[256,2]{0,1:T(2,128)}, u32[]{:S(2)}) copy-start(s32[256,2]{0,1:T(2,128)} %param.22) | copy-start | bytes 6148
  80.3 128.4 %reduce-scatter.5.cloned.1.call-start = ((), (), s32[]{:S(2)}) async-start(), calls=%async_computation.9 | async-start | bytes 2621440 | tf_op jit(solution)/shard_map/reduce_scatter | solution.py:131
  161.8 0.7 copy-start.5
  163.0 1.3 copy-start.1
  178.5 35.6 %copy-start.6 = (s32[256,2]{0,1:T(2,128)S(1)}, s32[256,2]{0,1:T(2,128)}, u32[]{:S(2)}) copy-start(s32[256,2]{0,1:T(2,128)} %param.23) | copy-start | bytes 6148
  178.5 50.1 %copy-start.2 = (bf16[256,256]{1,0:T(8,128)(2,1)S(1)}, bf16[256,256]{1,0:T(8,128)(2,1)}, u32[]{:S(2)}) copy-start(bf16[256,256]{1,0:T(8,128)(2,1)} %reduce-scatter.3.cloned.1.call-done) | copy-start | bytes 393220
  208.6 20.0 %all-to-all-start.5 = ((bf16[8,128,256]{2,1,0:T(8,128)(2,1)}), bf16[8,128,256]{2,1,0:T(8,128)(2,1)S(1)}, u32[]{:S(2)}, u32[]{:S(2)}) async-start(bf16[8,128,256]{2,1,0:T(8,128)(2,1)} %bitcast.106), calls=%async_computation.7 | async-start | bytes 1048576 | tf_op jit(solution)/shard_map/all_to_all | solution.py:134
Sparse Core Ops, SparseCore 0:
  80.4 18.8 reduce-scatter.2
  178.7 29.9 reduce-scatter.4
where the time goes:
time: 237 us
  blocking collectives  89.1 us (38%)
  waiting for transfers between devices  75.8 us (32%)
  matrix products  31.5 us (13%)
  starting transfers between devices  16.4 us (7%)
  between operations  13.8 us (6%)
  local copies, waits for them, and re-layouts  5.34 us (2%)
  other arithmetic  4.61 us (2%)
    all_to_all x1, blocking collectives, body(): lax.all_to_all(outgoing, 'freq', split_axis=0, concat_axis=0, tiled=True)  54 us
    reduce_scatter x1, waiting for transfers between devices, body(): lax.psum_scatter(partial_out.astype(jnp.bfloat16), ('chan', 'expert'), sc...  30.1 us
    all_to_all x2, blocking collectives, across_slabs(): lax.all_to_all(values.astype(jnp.bfloat16), 'freq', split_axis=0, concat_...  21.2 us
    dot_general x5, matrix products, matmul(): return jnp.dot(left, right, preferred_element_type=jnp.float32)  18.6 us
    reduce_scatter x1, waiting for transfers between devices, body(): lax.psum_scatter(matmul(hidden, mlp_down).astype(jnp.bfloat16), ('chan',...  16.4 us
    all_to_all x2, waiting for transfers between devices, across_slabs(): lax.all_to_all(values.astype(jnp.bfloat16), 'freq', split_axis=0, concat_...  15.2 us
    all_to_all x1, waiting for transfers between devices, body(): lax.all_to_all(expert_out, 'freq', split_axis=0, concat_axis=0, tiled=True)  14 us
    dot_general x12, matrix products, precise(): jnp.dot(left, right, precision=HIGH, preferred_element_type=jnp.float32)  11.8 us
  transfers between devices with their start and end apart: 5, of which 5 were waited for; matrix products, arithmetic and copies ran while one was open for 1% of the time, Pallas kernels for 0%

commit v1 on v0

--- a/solution.py
+++ b/solution.py
@@ -5,7 +5,6 @@
 from jax import lax
 from jax.sharding import PartitionSpec as P
 
-HIGH = lax.Precision.HIGHEST
 EPS = 1e-06
 
 
@@ -17,7 +16,7 @@
 
 
 def precise(left, right):
-    return jnp.dot(left, right, precision=HIGH, preferred_element_type=jnp.float32)
+    return matmul(left.astype(jnp.bfloat16), right.astype(jnp.bfloat16))
 
 
 def matmul(left, right):
@@ -114,17 +113,19 @@
     slots_all = slabs * capacity
     picks = routes.reshape(-1)
     onehot = (picks[:, None] == lax.broadcasted_iota(jnp.int32, (1, slabs), 1)).astype(jnp.int32)
-    earlier = jnp.cumsum(onehot, axis=0) - onehot
-    position = jnp.sum(earlier * onehot, axis=1)
+    order = lax.broadcasted_iota(jnp.int32, (picks.shape[0], picks.shape[0]), 0)
+    before = order > lax.broadcasted_iota(jnp.int32, order.shape, 1)
+    earlier = matmul(before.astype(jnp.bfloat16), onehot.astype(jnp.bfloat16))
+    position = jnp.sum(earlier.astype(jnp.int32) * onehot, axis=1)
     slot_ids = picks * capacity + position
     placed = lax.broadcasted_iota(jnp.int32, (slots_all, 1), 0) == slot_ids[None, :]
     placed = placed.reshape(slots_all, length, 2)
     send_table = jnp.any(placed, axis=2).astype(jnp.bfloat16)
     shares = combine.astype(jnp.float32) / 8.0
     merge_table = jnp.sum(jnp.where(placed, shares[None], 0.0), axis=2).astype(jnp.bfloat16)
-    whole_rows = lax.all_gather(encoded_half, ("chan", "expert"), axis=1, tiled=True)
-    outgoing = matmul(send_table, whole_rows).astype(jnp.bfloat16)
+    outgoing = matmul(send_table, encoded_half).astype(jnp.bfloat16)
     arrived = lax.all_to_all(outgoing, "freq", split_axis=0, concat_axis=0, tiled=True)
+    arrived = lax.all_gather(arrived, ("chan", "expert"), axis=1, tiled=True)
     expert_in = rms_rows(arrived, expert_gain)
     expert_hidden = gated(expert_in, expert_gate[0], expert_up[0])
     partial_out = matmul(expert_hidden, expert_down[0])

time: 237 us -> 216 us (0.911)
  blocking collectives: 89.1 us -> 48.5 us
  waiting for transfers between devices: 75.8 us -> 99.6 us
    all_to_all x1, blocking collectives: 54 us -> 20 us  [body(): lax.all_to_all(outgoing, 'freq', split_axis=0, concat_axis=0, tiled=True)]
    all_gather x0 -> x1, waiting for transfers between devices: none -> 21 us  [body(): arrived = lax.all_gather(arrived, ('chan', 'expert'), axis=1, tiled=True)]
    dot_general x12 -> x0, matrix products: 11.8 us -> none  [precise(): jnp.dot(left, right, precision=HIGH, preferred_element_type=jnp.float32)]
    dot_general x5 -> x18, matrix products: 18.6 us -> 29.7 us  [matmul(): return jnp.dot(left, right, preferred_element_type=jnp.float32)]
    all_gather x1 -> x0, blocking collectives: 6.79 us -> none  [body(): lax.all_gather(encoded_half, ('chan', 'expert'), axis=1, tiled=True)]
  transfers between devices with their start and end apart: 5 -> 6, of which waited for: 5 -> 6; matrix products, arithmetic and copies ran while one was open for 1% -> 1% of each run, Pallas kernels for 0% -> 0%
where the time goes in v1:
time: 216 us
  waiting for transfers between devices  99.6 us (46%)
  blocking collectives  48.5 us (22%)
  matrix products  30.7 us (14%)
  starting transfers between devices  16.5 us (8%)
  between operations  13.4 us (6%)
  other arithmetic  3.6 us (2%)
  local copies, waits for them, and re-layouts  3.47 us (2%)
    reduce_scatter x1, waiting for transfers between devices, body(): lax.psum_scatter(partial_out.astype(jnp.bfloat16), ('chan', 'expert'), sc...  31.6 us
    dot_general x18, matrix products, matmul(): return jnp.dot(left, right, preferred_element_type=jnp.float32)  29.7 us
    all_to_all x2, blocking collectives, across_slabs(): lax.all_to_all(values.astype(jnp.bfloat16), 'freq', split_axis=0, concat_...  21.2 us
    all_gather x1, waiting for transfers between devices, body(): arrived = lax.all_gather(arrived, ('chan', 'expert'), axis=1, tiled=True)  21 us
    all_to_all x1, blocking collectives, body(): lax.all_to_all(outgoing, 'freq', split_axis=0, concat_axis=0, tiled=True)  20 us
    reduce_scatter x1, waiting for transfers between devices, body(): lax.psum_scatter(matmul(hidden, mlp_down).astype(jnp.bfloat16), ('chan',...  17.7 us
    all_to_all x2, waiting for transfers between devices, across_slabs(): lax.all_to_all(values.astype(jnp.bfloat16), 'freq', split_axis=0, concat_...  15.2 us
    all_to_all x1, waiting for transfers between devices, body(): lax.all_to_all(expert_out, 'freq', split_axis=0, concat_axis=0, tiled=True)  14 us
  transfers between devices with their start and end apart: 6, of which 6 were waited for; matrix products, arithmetic and copies ran while one was open for 1% of the time, Pallas kernels for 0%

profile of v1, /device:TPU:0, one launch (start us, length us, event | category | flops | bytes accessed | tf_op | source)
XLA Modules:
  0.0 215.8 jit_solution(2628757277972654894)
XLA Ops:
  6.5 7.4 %all-to-all-start = ((bf16[8,32,256]{2,1,0:T(8,128)(2,1)}), bf16[8,32,256]{2,1,0:T(8,128)(2,1)S(1)}, u32[]{:S(2)}, u32[]{:S(2)}) async-start(bf16[8,32,256]{2,1,0:T(8,128)(2,1)} %bitcast.89), calls=%async_computation | async-start | bytes 262144 | tf_op jit(solution)/shard_map/all_to_all | solution.py:37
  14.1 7.2 %all-to-all-done = bf16[8,32,256]{2,1,0:T(8,128)(2,1)S(1)} async-done(((bf16[8,32,256]{2,1,0:T(8,128)(2,1)}), bf16[8,32,256]{2,1,0:T(8,128)(2,1)S(1)}, u32[]{:S(2)}, u32[]{:S(2)}) %all-to-all-start) | async-done | bytes 131104 | tf_op jit(solution)/shard_map/all_to_all | solution.py:37
  21.9 1.0 copy.62
  22.9 3.4 %all-to-all-start.1 = ((bf16[256,2,256]{2,1,0:T(2,128)(2,1)}), bf16[256,2,256]{2,1,0:T(2,128)(2,1)S(1)}, u32[]{:S(2)}, u32[]{:S(2)}) async-start(bf16[256,2,256]{2,1,0:T(2,128)(2,1)} %copy.62), calls=%async_computation.1 | async-start | bytes 524288 | tf_op jit(solution)/shard_map/all_to_all | solution.py:37
  26.4 8.1 %all-to-all-done.1 = bf16[256,2,256]{2,1,0:T(2,128)(2,1)S(1)} async-done(((bf16[256,2,256]{2,1,0:T(2,128)(2,1)}), bf16[256,2,256]{2,1,0:T(2,128)(2,1)S(1)}, u32[]{:S(2)}, u32[]{:S(2)}) %all-to-all-start.1) | async-done | bytes 262176 | tf_op jit(solution)/shard_map/all_to_all | solution.py:37
  34.8 1.1 fusion.53
  35.9 1.1 fusion.52
  37.0 1.1 convolution_add_fusion.1
  38.1 1.1 fusion.34
  39.2 1.2 fusion.50
  40.5 1.2 fusion.51
  41.7 1.3 convolution_add_fusion
  43.0 1.1 fusion.48
  44.4 11.2 %all_to_all.52 = bf16[256,2,256]{2,1,0:T(2,128)(2,1)S(1)} all-to-all(bf16[256,2,256]{2,1,0:T(2,128)(2,1)S(1)} %copy.65), channel_id=1, replica_groups=mesh['freq'=8,'chan'=2,'expert'=2] {'freq'}, dimensions={0} | all-to-all | bytes 524288 | tf_op jit(solution)/shard_map/all_to_all | solution.py:37
  55.6 1.1 slice_reduce_fusion
  57.4 10.0 %all_to_all.53 = bf16[8,32,256]{2,1,0:T(8,128)(2,1)S(1)} all-to-all(bf16[8,32,256]{2,1,0:T(8,128)(2,1)S(1)} %copy.68), channel_id=1, replica_groups=mesh['freq'=8,'chan'=2,'expert'=2] {'freq'}, dimensions={0} | all-to-all | bytes 262144 | tf_op jit(solution)/shard_map/all_to_all | solution.py:37
  67.5 7.4 %all_gather.6 = bf16[256,1024]{1,0:T(8,128)(2,1)S(1)} all-gather(bf16[256,256]{1,0:T(8,128)(2,1)S(1)} %get-tuple-element.7), channel_id=1, replica_groups=mesh['freq'=8,'chan'=2,'expert'=2] {'chan','expert'}, dimensions={1}, use_global_device_ids=true | all-gather | bytes 655360 | tf_op jit(solution)/shard_map/all_gather | solution.py:99
  75.0 0.5 fusion.45
  75.5 3.2 %convolution_convert_fusion = bf16[256,1024]{1,0:T(8,128)(2,1)} fusion(bf16[512,1024]{1,0:T(8,128)(2,1)} %param.17, bf16[1024,512]{1,0:T(8,128)(2,1)} %param.16, f32[256,512]{1,0:T(8,128)S(1)} %fusion.45, bf16[256,1024]{1,0:T(8,128)(2,1)S(1)} %all_gather.6, f32[1024]{0:T(1024)S(1)} %copy-done.8, f32[256]{0:T(256)S(1)} %add_rsqrt_fusion.1), kind=kOutput, calls=%fused_computation.19 | convolution fusion | flops 538968064 | bytes 3675136 | tf_op jit(solution)/shard_map/dot_general | solution.py:23
  79.6 0.4 fusion.9
  80.0 17.7 %reduce-scatter.3.cloned.1.call-done = bf16[256,256]{1,0:T(8,128)(2,1)} async-done(((bf16[256,1024]{1,0:T(8,128)(2,1)}), bf16[256,256]{1,0:T(8,128)(2,1)}) %reduce-scatter.3.cloned.1.call-update) | async-done | bytes 131088 | tf_op jit(solution)/shard_map/reduce_scatter | solution.py:103
  97.7 1.2 convolution_convert_fusion.1
  99.0 20.0 %all_to_all.54 = bf16[8,128,256]{2,1,0:T(8,128)(2,1)} all-to-all(bf16[8,128,256]{2,1,0:T(8,128)(2,1)S(1)} %bitcast.84), channel_id=1, replica_groups=mesh['freq'=8,'chan'=2,'expert'=2] {'freq'}, dimensions={0} | all-to-all | bytes 1048576 | tf_op jit(solution)/shard_map/all_to_all | solution.py:127
  119.0 21.0 %all-gather.2.cloned.1.call-done = bf16[1024,1024]{1,0:T(8,128)(2,1)} async-done(((bf16[1024,256]{1,0:T(8,128)(2,1)}), bf16[1024,1024]{1,0:T(8,128)(2,1)}) %all-gather.2.cloned.1.call-update) | async-done | bytes 2097168 | tf_op jit(solution)/shard_map/all_gather | solution.py:128
  140.0 2.2 %fusion.1 = f32[1024]{0:T(1024)S(1)} fusion(bf16[1024,1024]{1,0:T(8,128)(2,1)} %all-gather.2.cloned.1.call-done), kind=kLoop, calls=%fused_computation.4 | loop fusion | flops 3144704 | bytes 2101248 | tf_op jit(solution)/shard_map/reduce_sum | solution.py:28
  142.3 4.3 %fusion.7 = f32[1024,1024]{1,0:T(8,128)} fusion(bf16[1,1024,1024]{2,1,0:T(8,128)(2,1)S(1)} %copy-done, bf16[1024,1024]{1,0:T(8,128)(2,1)S(1)} %copy-done.1, f32[1024]{0:T(1024)S(1)} %copy-done.9, f32[1024]{0:T(1024)S(1)} %add_rsqrt_fusion), kind=kOutput, calls=%fused_computation.11 | convolution fusion | flops 2151677952 | bytes 8396800 | tf_op jit(solution)/shard_map/dot_general | solution.py:23
  146.6 10.0 %fusion.10 = bf16[1024,1024]{1,0:T(8,128)(2,1)} fusion(bf16[1,1024,1024]{2,1,0:T(8,128)(2,1)} %param.21, f32[1024,1024]{1,0:T(8,128)} %fusion.7, bf16[1,1024,1024]{2,1,0:T(8,128)(2,1)} %param.20, bf16[1024,1024]{1,0:T(8,128)(2,1)} %all-gather.2.cloned.1.call-done, f32[1024]{0:T(1024)S(1)} %copy-done.9, f32[1024]{0:T(1024)S(1)} %add_rsqrt_fusion), kind=kOutput, calls=%fused_computation.16 | convolution fusion | flops 4306501632 | bytes 12591104 | tf_op jit(solution)/shard_map/dot_general | solution.py:23
  156.6 31.6 %reduce-scatter.5.cloned.1.call-done = bf16[1024,256]{1,0:T(8,128)(2,1)} async-done(((bf16[1024,1024]{1,0:T(8,128)(2,1)}), bf16[1024,256]{1,0:T(8,128)(2,1)}) %reduce-scatter.5.cloned.1.call-update) | async-done | bytes 524304 | tf_op jit(solution)/shard_map/reduce_scatter | solution.py:132
  188.2 5.5 %all-to-all-start.5 = ((bf16[8,128,256]{2,1,0:T(8,128)(2,1)}), bf16[8,128,256]{2,1,0:T(8,128)(2,1)S(1)}, u32[]{:S(2)}, u32[]{:S(2)}) async-start(bf16[8,128,256]{2,1,0:T(8,128)(2,1)} %bitcast.88), calls=%async_computation.7 | async-start | bytes 1048576 | tf_op jit(solution)/shard_map/all_to_all | solution.py:135
  193.7 0.5 select_reduce_fusion
  194.2 14.0 %all-to-all-done.5 = bf16[8,128,256]{2,1,0:T(8,128)(2,1)S(1)} async-done(((bf16[8,128,256]{2,1,0:T(8,128)(2,1)}), bf16[8,128,256]{2,1,0:T(8,128)(2,1)S(1)}, u32[]{:S(2)}, u32[]{:S(2)}) %all-to-all-start.5) | async-done | bytes 524320 | tf_op jit(solution)/shard_map/all_to_all | solution.py:135
  208.2 1.0 fusion.16
  (54 shorter events, 3.3 us)
Async XLA Ops:
  6.5 135.7 %copy-start = (bf16[1,1024,1024]{2,1,0:T(8,128)(2,1)S(1)}, bf16[1,1024,1024]{2,1,0:T(8,128)(2,1)}, u32[]{:S(2)}) copy-start(bf16[1,1024,1024]{2,1,0:T(8,128)(2,1)} %param.19) | copy-start | bytes 6291460
  6.5 14.8 %all-to-all-start = ((bf16[8,32,256]{2,1,0:T(8,128)(2,1)}), bf16[8,32,256]{2,1,0:T(8,128)(2,1)S(1)}, u32[]{:S(2)}, u32[]{:S(2)}) async-start(bf16[8,32,256]{2,1,0:T(8,128)(2,1)} %bitcast.89), calls=%async_computation | async-start | bytes 262144 | tf_op jit(solution)/shard_map/all_to_all | solution.py:37
  22.9 11.6 %all-to-all-start.1 = ((bf16[256,2,256]{2,1,0:T(2,128)(2,1)}), bf16[256,2,256]{2,1,0:T(2,128)(2,1)S(1)}, u32[]{:S(2)}, u32[]{:S(2)}) async-start(bf16[256,2,256]{2,1,0:T(2,128)(2,1)} %copy.62), calls=%async_computation.1 | async-start | bytes 524288 | tf_op jit(solution)/shard_map/all_to_all | solution.py:37
  26.3 71.5 %reduce-scatter.3.cloned.1.call-start = ((), (), s32[]{:S(2)}) async-start(), calls=%async_computation.8 | async-start | bytes 655360 | tf_op jit(solution)/shard_map/reduce_scatter | solution.py:103
  34.8 3.3 %copy-start.7 = (bf16[2,256,1,256]{3,1,2,0:T(8,128)(2,1)S(1)}, bf16[2,256,1,256]{3,1,2,0:T(8,128)(2,1)}, u32[]{:S(2)}) copy-start(bf16[2,256,1,256]{3,1,2,0:T(8,128)(2,1)} %param.13) | copy-start | bytes 786436
  44.1 23.3 %copy-start.3 = (bf16[256,256]{1,0:T(8,128)(2,1)S(1)}, bf16[256,256]{1,0:T(8,128)(2,1)}, u32[]{:S(2)}) copy-start(bf16[256,256]{1,0:T(8,128)(2,1)} %param.12) | copy-start | bytes 393220
  56.8 18.2 %copy-start.6 = (bf16[1024,512]{1,0:T(8,128)(2,1)S(1)}, bf16[1024,512]{1,0:T(8,128)(2,1)}, u32[]{:S(2)}) copy-start(bf16[1024,512]{1,0:T(8,128)(2,1)} %param.15) | copy-start | bytes 3145732
  56.8 18.2 %copy-start.8 = (f32[1024]{0:T(1024)S(1)}, f32[1024]{0:T(1024)}, u32[]{:S(2)}) copy-start(f32[1024]{0:T(1024)} %param.14) | copy-start | bytes 12292
  75.5 3.3 %copy-start.4 = (s32[256,2]{0,1:T(2,128)S(1)}, s32[256,2]{0,1:T(2,128)}, u32[]{:S(2)}) copy-start(s32[256,2]{0,1:T(2,128)} %param.22) | copy-start | bytes 6148
  78.8 61.2 %all-gather.2.cloned.1.call-start = ((), (), s32[]{:S(2)}) async-start(), calls=%async_computation.9 | async-start | bytes 2621440 | tf_op jit(solution)/shard_map/all_gather | solution.py:128
  99.0 43.3 %copy-start.9 = (f32[1024]{0:T(1024)S(1)}, f32[1024]{0:T(1024)}, u32[]{:S(2)}) copy-start(f32[1024]{0:T(1024)} %param.18) | copy-start | bytes 12292
  118.9 69.2 %reduce-scatter.5.cloned.1.call-start = ((), (), s32[]{:S(2)}) async-start(), calls=%async_computation.10 | async-start | bytes 2621440 | tf_op jit(solution)/shard_map/reduce_scatter | solution.py:132
  140.0 2.3 %copy-start.1 = (bf16[1024,1024]{1,0:T(8,128)(2,1)S(1)}, bf16[1024,1024]{1,0:T(8,128)(2,1)}, u32[]{:S(2)}) copy-start(bf16[1024,1024]{1,0:T(8,128)(2,1)} %all-gather.2.cloned.1.call-done) | copy-start | bytes 6291460
  156.6 37.1 %copy-start.5 = (s32[256,2]{0,1:T(2,128)S(1)}, s32[256,2]{0,1:T(2,128)}, u32[]{:S(2)}) copy-start(s32[256,2]{0,1:T(2,128)} %param.23) | copy-start | bytes 6148
  156.6 51.6 %copy-start.2 = (bf16[256,256]{1,0:T(8,128)(2,1)S(1)}, bf16[256,256]{1,0:T(8,128)(2,1)}, u32[]{:S(2)}) copy-start(bf16[256,256]{1,0:T(8,128)(2,1)} %reduce-scatter.3.cloned.1.call-done) | copy-start | bytes 393220
  188.2 20.0 %all-to-all-start.5 = ((bf16[8,128,256]{2,1,0:T(8,128)(2,1)}), bf16[8,128,256]{2,1,0:T(8,128)(2,1)S(1)}, u32[]{:S(2)}, u32[]{:S(2)}) async-start(bf16[8,128,256]{2,1,0:T(8,128)(2,1)} %bitcast.88), calls=%async_computation.7 | async-start | bytes 1048576 | tf_op jit(solution)/shard_map/all_to_all | solution.py:135
Sparse Core Ops, SparseCore 0:
  78.9 18.7 reduce-scatter.2
  119.1 20.9 all-gather.1
  156.8 31.3 reduce-scatter.4

commit v2 on v1

--- a/solution.py
+++ b/solution.py
@@ -1,8 +1,11 @@
+import functools
 import math
 
 import jax
 import jax.numpy as jnp
 from jax import lax
+from jax.experimental import pallas as pl
+from jax.experimental.pallas import tpu as pltpu
 from jax.sharding import PartitionSpec as P
 
 EPS = 1e-06
@@ -78,6 +81,299 @@
     spatial = precise(cos_slab, real_rows) - precise(sin_slab, imag_rows)
     spatial = spatial.reshape(length, channels)
     return across_slabs(spatial) / length_all
+
+
+def experts_kernel(
+    slabs,
+    per,
+    out_ref_rows,
+    gain_ref,
+    gate_hbm,
+    up_hbm,
+    down_hbm,
+    back_ref,
+    gate_ref,
+    up_ref,
+    down_ref,
+    rows_ref,
+    normed_ref,
+    hidden_ref,
+    part_ref,
+    pair_ref,
+    turn_ref,
+    cross_ref,
+    final_ref,
+    ret_ref,
+    weight_sem,
+    disp_send,
+    disp_recv,
+    x_send,
+    x_recv,
+    sib_send,
+    sib_recv,
+    fwd_send,
+    fwd_recv,
+    pair_send,
+    pair_recv,
+    cross_send,
+    cross_recv,
+    ret_send,
+    ret_recv,
+):
+    me = lax.axis_index("freq")
+    chan = lax.axis_index("chan")
+    core = lax.axis_index("expert")
+    mine = chan * 2 + core
+    other = (1 - chan) * 2 + core
+    groups = slabs // per
+    capacity, width = rows_ref.shape[2], rows_ref.shape[3]
+    rows = per * capacity
+
+    loads = [
+        pltpu.make_async_copy(source, target, weight_sem.at[number])
+        for number, (source, target) in enumerate(
+            ((gate_hbm, gate_ref), (up_hbm, up_ref), (down_hbm, down_ref))
+        )
+    ]
+    for load in loads:
+        load.start()
+
+    barrier = pltpu.get_barrier_semaphore()
+    for k in range(1, slabs):
+        pl.semaphore_signal(
+            barrier, inc=1, device_id={"freq": lax.rem(me + k, slabs)}, device_id_type=pl.DeviceIdType.MESH
+        )
+    pl.semaphore_signal(barrier, inc=1, device_id={"chan": 1 - chan}, device_id_type=pl.DeviceIdType.MESH)
+    pl.semaphore_signal(barrier, inc=1, device_id={"expert": 1 - core}, device_id_type=pl.DeviceIdType.MESH)
+    pl.semaphore_wait(barrier, slabs + 1)
+
+    def remote(source, target, send, recv, device):
+        return pltpu.make_async_remote_copy(
+            src_ref=source,
+            dst_ref=target,
+            send_sem=send,
+            recv_sem=recv,
+            device_id=device,
+            device_id_type=pl.DeviceIdType.MESH,
+        )
+
+    def dispatch(k):
+        peer = lax.rem(me + k, slabs)
+        return remote(
+            out_ref_rows.at[peer], rows_ref.at[mine, k], disp_send.at[k], disp_recv.at[k], {"freq": peer}
+        )
+
+    def span(i):
+        return pl.ds(i * per, per)
+
+    def to_cross(i):
+        block = rows_ref.at[mine, span(i)]
+        return remote(block, block, x_send.at[i], x_recv.at[i], {"chan": 1 - chan})
+
+    def from_cross(i):
+        block = rows_ref.at[other, span(i)]
+        return remote(block, block, x_send.at[i], x_recv.at[i], {"chan": 1 - chan})
+
+    def to_sibling(i):
+        block = rows_ref.at[mine, span(i)]
+        return remote(block, block, sib_send.at[i], sib_recv.at[i], {"expert": 1 - core})
+
+    def forward(i):
+        block = rows_ref.at[other, span(i)]
+        return remote(block, block, fwd_send.at[i], fwd_recv.at[i], {"expert": 1 - core})
+
+    def pair(c, i):
+        return remote(
+            part_ref.at[c * 2 + 1 - core, span(i)],
+            pair_ref.at[c, span(i)],
+            pair_send.at[c, i],
+            pair_recv.at[c, i],
+            {"expert": 1 - core},
+        )
+
+    def cross(i):
+        return remote(
+            turn_ref.at[span(i)], cross_ref.at[span(i)], cross_send.at[i], cross_recv.at[i], {"chan": 1 - chan}
+        )
+
+    def give_back(k):
+        home = lax.rem(me - k + slabs, slabs)
+        return remote(final_ref.at[k], ret_ref.at[k], ret_send.at[k], ret_recv.at[k], {"freq": home})
+
+    def arrive(i):
+        for j in range(per):
+            k = i * per + j
+
+            @pl.when(k > 0)
+            def _():
+                dispatch(k).wait_recv()
+
+        to_cross(i).start()
+        to_sibling(i).start()
+
+    def pass_on(i):
+        from_cross(i).wait_recv()
+        forward(i).start()
+
+    def compute(i):
+        to_sibling(i).wait_recv()
+        forward(i).wait_recv()
+        quarters = [
+            rows_ref[q, span(i)].reshape(rows, width).astype(jnp.float32) for q in range(4)
+        ]
+        total = sum(jnp.sum(x * x, axis=-1, keepdims=True) for x in quarters)
+        scale = lax.rsqrt(total / (4 * width) + EPS)
+        for q in range(4):
+            cols = slice(q * width, (q + 1) * width)
+            normed_ref[:, cols] = (quarters[q] * scale * gain_ref[:, cols]).astype(jnp.bfloat16)
+
+        @pl.when(i == 0)
+        def _():
+            for load in loads:
+                load.wait()
+
+        tile = 256
+        for start in range(0, hidden_ref.shape[1], tile):
+            cols = slice(start, start + tile)
+            gate = matmul(normed_ref[...], gate_ref[0, :, cols])
+            up = matmul(normed_ref[...], up_ref[0, :, cols])
+            hidden_ref[:, cols] = (gate / (1.0 + jnp.exp(-gate)) * up).astype(jnp.bfloat16)
+        for q in range(4):
+            part = matmul(hidden_ref[...], down_ref[0, :, q * width : (q + 1) * width])
+            part_ref[q, span(i)] = part.astype(jnp.bfloat16).reshape(per, capacity, width)
+        pair(0, i).start()
+        pair(1, i).start()
+
+    def both(q, c, i):
+        return part_ref[q, span(i)].astype(jnp.float32) + pair_ref[c, span(i)].astype(jnp.float32)
+
+    def turn(i):
+        pair(0, i).wait_recv()
+        pair(1, i).wait_recv()
+        turn_ref[span(i)] = both(other, 1 - chan, i).astype(jnp.bfloat16)
+        cross(i).start()
+
+    def finish(i):
+        cross(i).wait_recv()
+        final_ref[span(i)] = (both(mine, chan, i) + cross_ref[span(i)].astype(jnp.float32)).astype(
+            jnp.bfloat16
+        )
+        for j in range(per):
+            k = i * per + j
+
+            @pl.when(k > 0)
+            def _():
+                give_back(k).start()
+
+    for k in range(1, slabs):
+        dispatch(k).start()
+    rows_ref[mine, 0] = out_ref_rows[me]
+    arrive(0)
+    pass_on(0)
+
+    def step(i, carry):
+        @pl.when(i + 1 < groups)
+        def _():
+            arrive(i + 1)
+
+        compute(i)
+
+        @pl.when(i + 1 < groups)
+        def _():
+            pass_on(i + 1)
+
+        @pl.when(i >= 1)
+        def _():
+            turn(i - 1)
+
+        @pl.when(i >= 2)
+        def _():
+            finish(i - 2)
+
+        return carry
+
+    lax.fori_loop(0, groups, step, 0)
+    turn(groups - 1)
+    if groups >= 2:
+        finish(groups - 2)
+    finish(groups - 1)
+    back_ref[me] = final_ref[0]
+    for k in range(1, slabs):
+        give_back(k).wait_recv()
+        back_ref[lax.rem(me + k, slabs)] = ret_ref[k]
+    for k in range(1, slabs):
+        dispatch(k).wait_send()
+        give_back(k).wait_send()
+    for i in range(groups):
+        to_cross(i).wait_send()
+        to_sibling(i).wait_send()
+        forward(i).wait_send()
+        pair(0, i).wait_send()
+        pair(1, i).wait_send()
+        cross(i).wait_send()
+
+
+def experts_direct(outgoing, gain, gate_w, up_w, down_w):
+    slabs, capacity, width = outgoing.shape
+    per = max(1, 256 // capacity)
+    groups = slabs // per
+    hidden = gate_w.shape[2]
+    half = jnp.bfloat16
+    dma = pltpu.SemaphoreType.DMA
+    vmem = pl.BlockSpec(memory_space=pltpu.VMEM)
+    hbm = pl.BlockSpec(memory_space=pl.ANY)
+    return pl.pallas_call(
+        functools.partial(experts_kernel, slabs, per),
+        out_shape=jax.ShapeDtypeStruct(outgoing.shape, half),
+        in_specs=[vmem, vmem, hbm, hbm, hbm],
+        out_specs=vmem,
+        scratch_shapes=[
+            pltpu.VMEM(gate_w.shape, half),
+            pltpu.VMEM(up_w.shape, half),
+            pltpu.VMEM(down_w.shape, half),
+            pltpu.VMEM((4, slabs, capacity, width), half),
+            pltpu.VMEM((per * capacity, 4 * width), half),
+            pltpu.VMEM((per * capacity, hidden), half),
+            pltpu.VMEM((4, slabs, capacity, width), half),
+            pltpu.VMEM((2, slabs, capacity, width), half),
+            pltpu.VMEM((slabs, capacity, width), half),
+            pltpu.VMEM((slabs, capacity, width), half),
+            pltpu.VMEM((slabs, capacity, width), half),
+            pltpu.VMEM((slabs, capacity, width), half),
+            dma((3,)),
+            dma((slabs,)),
+            dma((slabs,)),
+            dma((groups,)),
+            dma((groups,)),
+            dma((groups,)),
+            dma((groups,)),
+            dma((groups,)),
+            dma((groups,)),
+            dma((2, groups)),
+            dma((2, groups)),
+            dma((groups,)),
+            dma((groups,)),
+            dma((slabs,)),
+            dma((slabs,)),
+        ],
+        compiler_params=pltpu.CompilerParams(
+            collective_id=1, has_side_effects=True, vmem_limit_bytes=36 * 1024 * 1024
+        ),
+        cost_estimate=pl.CostEstimate(
+            flops=6 * slabs * capacity * 4 * width * hidden, bytes_accessed=3 * 8 * width * hidden, transcendentals=0
+        ),
+    )(outgoing, gain[None], gate_w, up_w, down_w)
+
+
+def experts_plain(outgoing, gain, gate_w, up_w, down_w):
+    slabs, capacity, width = outgoing.shape
+    arrived = lax.all_to_all(outgoing, "freq", split_axis=0, concat_axis=0, tiled=True)
+    arrived = lax.all_gather(arrived, ("chan", "expert"), axis=2, tiled=True).reshape(slabs * capacity, -1)
+    expert_hidden = gated(rms_rows(arrived, gain), gate_w[0], up_w[0])
+    expert_out = lax.psum_scatter(
+        matmul(expert_hidden, down_w[0]).astype(jnp.bfloat16), ("chan", "expert"), scatter_dimension=1, tiled=True
+    ).reshape(slabs, capacity, width)
+    return lax.all_to_all(expert_out, "freq", split_axis=0, concat_axis=0, tiled=True)
 
 
 def body(
@@ -124,15 +420,15 @@
     shares = combine.astype(jnp.float32) / 8.0
     merge_table = jnp.sum(jnp.where(placed, shares[None], 0.0), axis=2).astype(jnp.bfloat16)
     outgoing = matmul(send_table, encoded_half).astype(jnp.bfloat16)
-    arrived = lax.all_to_all(outgoing, "freq", split_axis=0, concat_axis=0, tiled=True)
-    arrived = lax.all_gather(arrived, ("chan", "expert"), axis=1, tiled=True)
-    expert_in = rms_rows(arrived, expert_gain)
-    expert_hidden = gated(expert_in, expert_gate[0], expert_up[0])
-    partial_out = matmul(expert_hidden, expert_down[0])
-    expert_out = lax.psum_scatter(
-        partial_out.astype(jnp.bfloat16), ("chan", "expert"), scatter_dimension=1, tiled=True
+    outgoing = outgoing.reshape(slabs, capacity, -1)
+    direct = (
+        lax.axis_size("chan") == 2
+        and lax.axis_size("expert") == 2
+        and capacity % 16 == 0
+        and slabs % max(1, 256 // capacity) == 0
     )
-    returned = lax.all_to_all(expert_out, "freq", split_axis=0, concat_axis=0, tiled=True)
+    experts = experts_direct if direct else experts_plain
+    returned = experts(outgoing, expert_gain, expert_gate, expert_up, expert_down).reshape(slots_all, -1)
     routed_sum = lax.dot_general(
         merge_table, returned, (((0,), (0,)), ((), ())), preferred_element_type=jnp.float32
     )

time: 216 us -> 161 us (0.75)
  waiting for transfers between devices: 99.6 us -> 30.3 us
  Pallas kernels: 0 us -> 49.8 us
  blocking collectives: 48.5 us -> 28.7 us
  matrix products: 30.7 us -> 16.8 us
  starting transfers between devices: 16.5 us -> 10.9 us
  local copies, waits for them, and re-layouts: 3.47 us -> 6.64 us
    pallas_call x0 -> x1, Pallas kernels: none -> 49.8 us  [experts_direct(): pl.pallas_call(functools.partial(experts_kernel, slabs, per), out_shape=j...]
    reduce_scatter x1 -> x0, waiting for transfers between devices: 31.6 us -> none  [body(): lax.psum_scatter(partial_out.astype(jnp.bfloat16), ('chan', 'expert'), sc...]
    all_gather x1 -> x0, waiting for transfers between devices: 21 us -> none  [body(): arrived = lax.all_gather(arrived, ('chan', 'expert'), axis=1, tiled=True)]
    all_to_all x1 -> x0, blocking collectives: 20 us -> none  [body(): lax.all_to_all(outgoing, 'freq', split_axis=0, concat_axis=0, tiled=True)]
    all_to_all x1 -> x0, waiting for transfers between devices: 14 us -> none  [body(): lax.all_to_all(expert_out, 'freq', split_axis=0, concat_axis=0, tiled=True)]
    dot_general x18 -> x16, matrix products: 29.7 us -> 15.8 us  [matmul(): return jnp.dot(left, right, preferred_element_type=jnp.float32)]
    all_to_all x1 -> x0, starting transfers between devices: 5.52 us -> none  [body(): lax.all_to_all(expert_out, 'freq', split_axis=0, concat_axis=0, tiled=True)]
    unnamed x23 -> x29, local copies, waits for them, and re-layouts: 0.34 us -> 3.52 us
  transfers between devices with their start and end apart: 6 -> 3, of which waited for: 6 -> 3; matrix products, arithmetic and copies ran while one was open for 1% -> 3% of each run, Pallas kernels for 0% -> 0%
where the time goes in v2:
time: 161 us; the launch traced here: 160 us
  Pallas kernels  49.8 us (31%)
  waiting for transfers between devices  30.3 us (19%)
  blocking collectives  28.7 us (18%)
  matrix products  16.8 us (10%)
  between operations  13.7 us (9%)
  starting transfers between devices  10.9 us (7%)
  local copies, waits for them, and re-layouts  6.64 us (4%)
  other arithmetic  3.65 us (2%)
    pallas_call x1, Pallas kernels, experts_direct(): pl.pallas_call(functools.partial(experts_kernel, slabs, per), out_shape=j...  49.8 us
    all_to_all x2, blocking collectives, across_slabs(): lax.all_to_all(values.astype(jnp.bfloat16), 'freq', split_axis=0, concat_...  21.2 us
    dot_general x16, matrix products, matmul(): return jnp.dot(left, right, preferred_element_type=jnp.float32)  15.8 us
    all_to_all x2, waiting for transfers between devices, across_slabs(): lax.all_to_all(values.astype(jnp.bfloat16), 'freq', split_axis=0, concat_...  15.2 us
    reduce_scatter x1, waiting for transfers between devices, body(): lax.psum_scatter(matmul(hidden, mlp_down).astype(jnp.bfloat16), ('chan',...  15 us
    all_to_all x2, starting transfers between devices, across_slabs(): lax.all_to_all(values.astype(jnp.bfloat16), 'freq', split_axis=0, concat_...  10.8 us
    all_gather x1, blocking collectives, body(): lax.all_gather(mixed_sum.astype(jnp.bfloat16), ('chan', 'expert'), axis=1...  7.48 us
    unnamed x29, local copies, waits for them, and re-layouts  3.52 us
  transfers between devices with their start and end apart: 3, of which 3 were waited for; matrix products, arithmetic and copies ran while one was open for 3% of the time, Pallas kernels for 0%

profile of v2, /device:TPU:0, one launch (start us, length us, event | category | flops | bytes accessed | tf_op | source)
XLA Modules:
  0.0 160.3 jit_solution(6480586437765382518)
XLA Ops:
  6.5 7.4 %all-to-all-start = ((bf16[8,32,256]{2,1,0:T(8,128)(2,1)}), bf16[8,32,256]{2,1,0:T(8,128)(2,1)S(1)}, u32[]{:S(2)}, u32[]{:S(2)}) async-start(bf16[8,32,256]{2,1,0:T(8,128)(2,1)} %bitcast.74), calls=%async_computation | async-start | bytes 262144 | tf_op jit(solution)/shard_map/all_to_all | solution.py:40
  14.1 7.2 %all-to-all-done = bf16[8,32,256]{2,1,0:T(8,128)(2,1)S(1)} async-done(((bf16[8,32,256]{2,1,0:T(8,128)(2,1)}), bf16[8,32,256]{2,1,0:T(8,128)(2,1)S(1)}, u32[]{:S(2)}, u32[]{:S(2)}) %all-to-all-start) | async-done | bytes 131104 | tf_op jit(solution)/shard_map/all_to_all | solution.py:40
  21.5 0.3 add_convert_fusion.1
  21.9 1.0 copy.62
  22.8 3.4 %all-to-all-start.1 = ((bf16[256,2,256]{2,1,0:T(2,128)(2,1)}), bf16[256,2,256]{2,1,0:T(2,128)(2,1)S(1)}, u32[]{:S(2)}, u32[]{:S(2)}) async-start(bf16[256,2,256]{2,1,0:T(2,128)(2,1)} %copy.62), calls=%async_computation.1 | async-start | bytes 524288 | tf_op jit(solution)/shard_map/all_to_all | solution.py:40
  26.4 8.1 %all-to-all-done.1 = bf16[256,2,256]{2,1,0:T(2,128)(2,1)S(1)} async-done(((bf16[256,2,256]{2,1,0:T(2,128)(2,1)}), bf16[256,2,256]{2,1,0:T(2,128)(2,1)S(1)}, u32[]{:S(2)}, u32[]{:S(2)}) %all-to-all-start.1) | async-done | bytes 262176 | tf_op jit(solution)/shard_map/all_to_all | solution.py:40
  34.4 0.4 fusion.112
  34.8 1.1 fusion.37
  35.9 1.1 fusion.36
  37.0 1.1 convolution_add_fusion.1
  38.1 1.1 fusion.18
  39.2 1.2 fusion.34
  40.5 1.2 fusion.35
  41.7 1.3 convolution_add_fusion
  43.0 1.1 fusion.32
  44.2 0.3 copy.65
  44.4 11.2 %all_to_all.28 = bf16[256,2,256]{2,1,0:T(2,128)(2,1)S(1)} all-to-all(bf16[256,2,256]{2,1,0:T(2,128)(2,1)S(1)} %copy.65), channel_id=1, replica_groups=mesh['freq'=8,'chan'=2,'expert'=2] {'freq'}, dimensions={0} | all-to-all | bytes 524288 | tf_op jit(solution)/shard_map/all_to_all | solution.py:40
  55.6 1.1 slice_reduce_fusion
  57.3 10.0 %all_to_all.29 = bf16[8,32,256]{2,1,0:T(8,128)(2,1)S(1)} all-to-all(bf16[8,32,256]{2,1,0:T(8,128)(2,1)S(1)} %copy.68), channel_id=1, replica_groups=mesh['freq'=8,'chan'=2,'expert'=2] {'freq'}, dimensions={0} | all-to-all | bytes 262144 | tf_op jit(solution)/shard_map/all_to_all | solution.py:40
  67.5 7.5 %all_gather.3 = bf16[256,1024]{1,0:T(8,128)(2,1)S(1)} all-gather(bf16[256,256]{1,0:T(8,128)(2,1)S(1)} %get-tuple-element.7), channel_id=1, replica_groups=mesh['freq'=8,'chan'=2,'expert'=2] {'chan','expert'}, dimensions={1}, use_global_device_ids=true | all-gather | bytes 655360 | tf_op jit(solution)/shard_map/all_gather | solution.py:395
  75.2 1.3 fusion.29
  76.4 2.7 %convolution_convert_fusion = bf16[256,1024]{1,0:T(8,128)(2,1)} fusion(bf16[512,1024]{1,0:T(8,128)(2,1)S(1)} %copy-done, bf16[1024,512]{1,0:T(8,128)(2,1)S(1)} %copy-done.10, f32[256,512]{1,0:T(8,128)} %fusion.29, bf16[256,1024]{1,0:T(8,128)(2,1)S(1)} %all_gather.3, f32[1024]{0:T(1024)S(1)} %copy-done.12, f32[256]{0:T(256)S(1)} %add_rsqrt_fusion), kind=kOutput, calls=%fused_computation.7 | convolution fusion | flops 538968064 | bytes 3675136 | tf_op jit(solution)/shard_map/dot_general | solution.py:26
  79.5 0.3 fusion.5
  80.0 1.2 fusion.1
  81.2 0.7 convert_multiply_fusion.7
  81.9 1.3 select_reduce_fusion
  83.1 15.0 %reduce-scatter.2.cloned.1.call-done = bf16[256,256]{1,0:T(8,128)(2,1)} async-done(((bf16[256,1024]{1,0:T(8,128)(2,1)}), bf16[256,256]{1,0:T(8,128)(2,1)}) %reduce-scatter.2.cloned.1.call-update) | async-done | bytes 131088 | tf_op jit(solution)/shard_map/reduce_scatter | solution.py:399
  98.2 1.3 convolution_convert_fusion.1
  99.5 1.6 copy-done.2
  101.1 1.6 copy-done.3
  102.7 49.8 %shard_map.118 = bf16[8,128,256]{2,1,0:T(8,128)(2,1)S(1)} custom-call(bf16[8,128,256]{2,1,0:T(8,128)(2,1)S(1)} %bitcast.68, f32[1,1024]{1,0:T(1,128)S(1)} %bitcast.69, bf16[1,1024,1024]{2,1,0:T(8,128)(2,1)S(1)} %copy-done.1, bf16[1,1024,1024]{2,1,0:T(8,128)(2,1)S(1)} %copy-done.2, bf16[1,1024,1024]{2,1,0:T(8,128)(2,1)S(1)} %copy-done.3), custom_call_target="tpu_custom_call" | custom-call | flops 6442450944 | bytes 6291456 | tf_op jit(solution)/shard_map/pallas_call | solution.py:325
  152.5 1.0 fusion.3
  (48 shorter events, 2.0 us)
Async XLA Ops:
  6.5 69.9 %copy-start = (bf16[512,1024]{1,0:T(8,128)(2,1)S(1)}, bf16[512,1024]{1,0:T(8,128)(2,1)}, u32[]{:S(2)}) copy-start(bf16[512,1024]{1,0:T(8,128)(2,1)} %param.17) | copy-start | bytes 3145732
  6.5 14.8 %all-to-all-start = ((bf16[8,32,256]{2,1,0:T(8,128)(2,1)}), bf16[8,32,256]{2,1,0:T(8,128)(2,1)S(1)}, u32[]{:S(2)}, u32[]{:S(2)}) async-start(bf16[8,32,256]{2,1,0:T(8,128)(2,1)} %bitcast.74), calls=%async_computation | async-start | bytes 262144 | tf_op jit(solution)/shard_map/all_to_all | solution.py:40
  22.8 11.6 %all-to-all-start.1 = ((bf16[256,2,256]{2,1,0:T(2,128)(2,1)}), bf16[256,2,256]{2,1,0:T(2,128)(2,1)S(1)}, u32[]{:S(2)}, u32[]{:S(2)}) async-start(bf16[256,2,256]{2,1,0:T(2,128)(2,1)} %copy.62), calls=%async_computation.1 | async-start | bytes 524288 | tf_op jit(solution)/shard_map/all_to_all | solution.py:40
  26.3 71.9 %reduce-scatter.2.cloned.1.call-start = ((), (), s32[]{:S(2)}) async-start(), calls=%async_computation.5 | async-start | bytes 655360 | tf_op jit(solution)/shard_map/reduce_scatter | solution.py:399
  34.8 3.3 %copy-start.11 = (bf16[2,256,1,256]{3,1,2,0:T(8,128)(2,1)S(1)}, bf16[2,256,1,256]{3,1,2,0:T(8,128)(2,1)}, u32[]{:S(2)}) copy-start(bf16[2,256,1,256]{3,1,2,0:T(8,128)(2,1)} %param.13) | copy-start | bytes 786436
  44.1 23.3 %copy-start.7 = (bf16[256,256]{1,0:T(8,128)(2,1)S(1)}, bf16[256,256]{1,0:T(8,128)(2,1)}, u32[]{:S(2)}) copy-start(bf16[256,256]{1,0:T(8,128)(2,1)} %param.12) | copy-start | bytes 393220
  56.8 18.4 %copy-start.9 = (bf16[1024,512]{1,0:T(8,128)(2,1)S(1)}, bf16[1024,512]{1,0:T(8,128)(2,1)}, u32[]{:S(2)}) copy-start(bf16[1024,512]{1,0:T(8,128)(2,1)} %param.15) | copy-start | bytes 3145732
  56.8 18.4 %copy-start.12 = (f32[1024]{0:T(1024)S(1)}, f32[1024]{0:T(1024)}, u32[]{:S(2)}) copy-start(f32[1024]{0:T(1024)} %param.14) | copy-start | bytes 12292
  67.4 9.0 %copy-start.10 = (bf16[1024,512]{1,0:T(8,128)(2,1)S(1)}, bf16[1024,512]{1,0:T(8,128)(2,1)}, u32[]{:S(2)}) copy-start(bf16[1024,512]{1,0:T(8,128)(2,1)} %param.16) | copy-start | bytes 3145732
  76.4 2.8 %copy-start.8 = (s32[256,2]{0,1:T(2,128)S(1)}, s32[256,2]{0,1:T(2,128)}, u32[]{:S(2)}) copy-start(s32[256,2]{0,1:T(2,128)} %param.22) | copy-start | bytes 6148
  79.2 20.3 %copy-start.1 = (bf16[1,1024,1024]{2,1,0:T(8,128)(2,1)S(1)}, bf16[1,1024,1024]{2,1,0:T(8,128)(2,1)}, u32[]{:S(2)}) copy-start(bf16[1,1024,1024]{2,1,0:T(8,128)(2,1)} %gate_hbm.1) | copy-start | bytes 6291460
  79.2 20.3 %copy-start.4 = (f32[1024]{0:T(1024)S(1)}, f32[1024]{0:T(1024)}, u32[]{:S(2)}) copy-start(f32[1024]{0:T(1024)} %param.18) | copy-start | bytes 12292
  99.5 1.6 copy-start.2
  101.1 1.6 copy-start.3
  102.7 49.8 %copy-start.5 = (bf16[1024,256]{1,0:T(8,128)(2,1)S(1)}, bf16[1024,256]{1,0:T(8,128)(2,1)}, u32[]{:S(2)}) copy-start(bf16[1024,256]{1,0:T(8,128)(2,1)} %select_reduce_fusion) | copy-start | bytes 1572868
  102.7 49.8 %copy-start.6 = (bf16[256,256]{1,0:T(8,128)(2,1)S(1)}, bf16[256,256]{1,0:T(8,128)(2,1)}, u32[]{:S(2)}) copy-start(bf16[256,256]{1,0:T(8,128)(2,1)} %reduce-scatter.2.cloned.1.call-done) | copy-start | bytes 393220
Sparse Core Ops, SparseCore 0:
  79.3 18.7 reduce-scatter.1

commit v3 on v2

--- a/solution.py
+++ b/solution.py
@@ -36,10 +36,53 @@
     return (jax.nn.silu(matmul(normed, gate_w)) * matmul(normed, up_w)).astype(jnp.bfloat16)
 
 
-def across_slabs(values):
-    return lax.all_to_all(
-        values.astype(jnp.bfloat16), "freq", split_axis=0, concat_axis=0, tiled=True
-    ).astype(values.dtype)
+def exchange_kernel(slabs, src_ref, dst_ref, land_ref, send_sem, recv_sem):
+    me = lax.axis_index("freq")
+    barrier = pltpu.get_barrier_semaphore()
+    for k in range(1, slabs):
+        pl.semaphore_signal(
+            barrier, inc=1, device_id={"freq": lax.rem(me + k, slabs)}, device_id_type=pl.DeviceIdType.MESH
+        )
+    pl.semaphore_wait(barrier, slabs - 1)
+    copies = []
+    for k in range(1, slabs):
+        peer = lax.rem(me + k, slabs)
+        copy = pltpu.make_async_remote_copy(
+            src_ref=src_ref.at[peer],
+            dst_ref=land_ref.at[k],
+            send_sem=send_sem.at[k],
+            recv_sem=recv_sem.at[k],
+            device_id={"freq": peer},
+            device_id_type=pl.DeviceIdType.MESH,
+        )
+        copy.start()
+        copies.append(copy)
+    dst_ref[me] = src_ref[me]
+    for k in range(1, slabs):
+        copies[k - 1].wait_recv()
+        dst_ref[lax.rem(me - k + slabs, slabs)] = land_ref[k]
+    for copy in copies:
+        copy.wait_send()
+
+
+def across_slabs(values, number):
+    slabs = values.shape[0]
+    values = values.astype(jnp.bfloat16)
+    if values.shape[1] % 16:
+        return lax.all_to_all(values, "freq", split_axis=0, concat_axis=0, tiled=True)
+    vmem = pl.BlockSpec(memory_space=pltpu.VMEM)
+    return pl.pallas_call(
+        functools.partial(exchange_kernel, slabs),
+        out_shape=jax.ShapeDtypeStruct(values.shape, jnp.bfloat16),
+        in_specs=[vmem],
+        out_specs=vmem,
+        scratch_shapes=[
+            pltpu.VMEM(values.shape, jnp.bfloat16),
+            pltpu.SemaphoreType.DMA((slabs,)),
+            pltpu.SemaphoreType.DMA((slabs,)),
+        ],
+        compiler_params=pltpu.CompilerParams(collective_id=number, has_side_effects=True),
+    )(values)
 
 
 def spectral_mix(signal, filter_pair):
@@ -51,7 +94,9 @@
     my_slab = lax.axis_index("freq")
     cos_slab, sin_slab = tables(slabs, slabs, slabs, 0)
     cos_long, sin_long = tables(length, length, length, 0)
-    gathered = across_slabs(signal).reshape(slabs, block_rows * channels)
+    gathered = across_slabs(signal.reshape(slabs, block_rows, channels), 2).reshape(
+        slabs, block_rows * channels
+    )
     first_re = precise(cos_slab, gathered).reshape(slabs, block_rows, channels)
     first_im = -precise(sin_slab, gathered).reshape(slabs, block_rows, channels)
     twist_cos, twist_sin = tables(slabs, block_rows, length_all, my_slab * block_rows)
@@ -59,10 +104,10 @@
     twist_sin = twist_sin[:, :, None]
     turned_re = first_re * twist_cos + first_im * twist_sin
     turned_im = first_im * twist_cos - first_re * twist_sin
-    packed = jnp.stack([turned_re, turned_im], axis=2).reshape(length, 2, channels)
-    columns = across_slabs(packed)
-    col_re = columns[:, 0]
-    col_im = columns[:, 1]
+    packed = jnp.concatenate([turned_re, turned_im], axis=1)
+    columns = across_slabs(packed, 3)
+    col_re = columns[:, :block_rows].reshape(length, channels)
+    col_im = columns[:, block_rows:].reshape(length, channels)
     freq_re = precise(cos_long, col_re) + precise(sin_long, col_im)
     freq_im = precise(cos_long, col_im) - precise(sin_long, col_re)
     coef_re = filter_pair[0, :, 0].astype(jnp.float32)
@@ -74,13 +119,14 @@
     undo_cos, undo_sin = tables(length, 1, length_all, my_slab)
     spun_re = back_re * undo_cos - back_im * undo_sin
     spun_im = back_im * undo_cos + back_re * undo_sin
-    packed_back = jnp.stack([spun_re, spun_im], axis=1)
-    rows_back = across_slabs(packed_back).reshape(slabs, block_rows, 2, channels)
-    real_rows = rows_back[:, :, 0].reshape(slabs, block_rows * channels)
-    imag_rows = rows_back[:, :, 1].reshape(slabs, block_rows * channels)
+    shape = (slabs, block_rows, channels)
+    packed_back = jnp.concatenate([spun_re.reshape(shape), spun_im.reshape(shape)], axis=1)
+    rows_back = across_slabs(packed_back, 4)
+    real_rows = rows_back[:, :block_rows].reshape(slabs, block_rows * channels)
+    imag_rows = rows_back[:, block_rows:].reshape(slabs, block_rows * channels)
     spatial = precise(cos_slab, real_rows) - precise(sin_slab, imag_rows)
-    spatial = spatial.reshape(length, channels)
-    return across_slabs(spatial) / length_all
+    spatial = across_slabs(spatial.reshape(shape), 5).reshape(length, channels)
+    return spatial.astype(jnp.float32) / length_all
 
 
 def experts_kernel(

time: 161 us -> 161 us (level)
  Pallas kernels: 49.8 us -> 90.4 us
  blocking collectives: 28.7 us -> 7.35 us
  waiting for transfers between devices: 30.3 us -> 18.2 us
  starting transfers between devices: 10.9 us -> 0.01 us
  other arithmetic: 3.65 us -> 6.05 us
    pallas_call x0 -> x4, Pallas kernels: none -> 40.8 us  [across_slabs(): pl.pallas_call(functools.partial(exchange_kernel, slabs), out_shape=jax.S...]
    all_to_all x2 -> x0, blocking collectives: 21.2 us -> none  [across_slabs(): lax.all_to_all(values.astype(jnp.bfloat16), 'freq', split_axis=0, concat_...]
    all_to_all x2 -> x0, waiting for transfers between devices: 15.2 us -> none  [across_slabs(): lax.all_to_all(values.astype(jnp.bfloat16), 'freq', split_axis=0, concat_...]
    all_to_all x2 -> x0, starting transfers between devices: 10.8 us -> none  [across_slabs(): lax.all_to_all(values.astype(jnp.bfloat16), 'freq', split_axis=0, concat_...]
    reduce_scatter x1, waiting for transfers between devices: 15 us -> 18.2 us  [body(): lax.psum_scatter(matmul(hidden, mlp_down).astype(jnp.bfloat16), ('chan',...]
    unnamed x29, local copies, waits for them, and re-layouts: 3.52 us -> 5.19 us
    dot_general x16, matrix products: 15.8 us -> 17.4 us  [matmul(): return jnp.dot(left, right, preferred_element_type=jnp.float32)]
  transfers between devices with their start and end apart: 3 -> 1, of which waited for: 3 -> 1; matrix products, arithmetic and copies ran while one was open for 3% -> 2% of each run, Pallas kernels for 0% -> 0%
where the time goes in v3:
time: 161 us
  Pallas kernels  90.4 us (56%)
  matrix products  18.4 us (11%)
  waiting for transfers between devices  18.2 us (11%)
  between operations  13.7 us (9%)
  blocking collectives  7.35 us (5%)
  local copies, waits for them, and re-layouts  6.58 us (4%)
  other arithmetic  6.05 us (4%)
    pallas_call x1, Pallas kernels, experts_direct(): pl.pallas_call(functools.partial(experts_kernel, slabs, per), out_shape=j...  49.6 us
    pallas_call x4, Pallas kernels, across_slabs(): pl.pallas_call(functools.partial(exchange_kernel, slabs), out_shape=jax.S...  40.8 us
    reduce_scatter x1, waiting for transfers between devices, body(): lax.psum_scatter(matmul(hidden, mlp_down).astype(jnp.bfloat16), ('chan',...  18.2 us
    dot_general x16, matrix products, matmul(): return jnp.dot(left, right, preferred_element_type=jnp.float32)  17.4 us
    all_gather x1, blocking collectives, body(): lax.all_gather(mixed_sum.astype(jnp.bfloat16), ('chan', 'expert'), axis=1...  7.35 us
    unnamed x29, local copies, waits for them, and re-layouts  5.19 us
  transfers between devices with their start and end apart: 1, of which 1 were waited for; matrix products, arithmetic and copies ran while one was open for 2% of the time, Pallas kernels for 0%

profile of v3, /device:TPU:0, one launch (start us, length us, event | category | flops | bytes accessed | tf_op | source)
XLA Modules:
  0.0 160.7 jit_solution(10847399300106554103)
XLA Ops:
  6.5 11.0 %shard_map.118 = bf16[8,32,256]{2,1,0:T(8,128)(2,1)} custom-call(bf16[8,32,256]{2,1,0:T(8,128)(2,1)} %bitcast.68), custom_call_target="tpu_custom_call" | custom-call | tf_op jit(solution)/shard_map/pallas_call | solution.py:74
  17.5 1.1 fusion.49
  18.6 1.1 fusion.51
  20.1 0.7 pad_maximum_fusion.src_ref
  20.8 10.4 %shard_map.119 = bf16[8,64,256]{2,1,0:T(8,128)(2,1)} custom-call(bf16[8,64,256]{2,1,0:T(8,128)(2,1)} %pad_maximum_fusion.src_ref), custom_call_target="tpu_custom_call" | custom-call | tf_op jit(solution)/shard_map/pallas_call | solution.py:74
  31.2 1.0 fusion.111
  32.3 1.3 fusion.35
  33.5 1.2 fusion.34
  34.8 1.3 convolution_add_fusion.1
  36.0 1.1 fusion.18
  37.2 1.2 fusion.33
  38.4 1.2 fusion.32
  39.6 1.3 convolution_subtract_fusion.1
  40.9 1.1 subtract_convert_fusion
  42.0 0.7 pad_maximum_fusion.1.src_ref
  42.7 10.2 %shard_map.120 = bf16[8,64,256]{2,1,0:T(8,128)(2,1)} custom-call(bf16[8,64,256]{2,1,0:T(8,128)(2,1)} %pad_maximum_fusion.1.src_ref), custom_call_target="tpu_custom_call" | custom-call | tf_op jit(solution)/shard_map/pallas_call | solution.py:74
  53.0 1.0 slice_bitcast_fusion
  54.6 0.7 copy.57
  55.3 9.2 %shard_map.121 = bf16[8,32,256]{2,1,0:T(8,128)(2,1)} custom-call(bf16[8,32,256]{2,1,0:T(8,128)(2,1)} %bitcast.67), custom_call_target="tpu_custom_call" | custom-call | tf_op jit(solution)/shard_map/pallas_call | solution.py:74
  64.5 0.9 convert_multiply_fusion.6
  65.5 7.4 %all_gather.3 = bf16[256,1024]{1,0:T(8,128)(2,1)S(1)} all-gather(bf16[256,256]{1,0:T(8,128)(2,1)S(1)} %get-tuple-element.5), channel_id=1, replica_groups=mesh['freq'=8,'chan'=2,'expert'=2] {'chan','expert'}, dimensions={1}, use_global_device_ids=true | all-gather | bytes 655360 | tf_op jit(solution)/shard_map/all_gather | solution.py:441
  73.0 0.5 fusion.29
  73.6 2.9 %convolution_convert_fusion = bf16[256,1024]{1,0:T(8,128)(2,1)} fusion(bf16[512,1024]{1,0:T(8,128)(2,1)S(1)} %copy-done, bf16[1024,512]{1,0:T(8,128)(2,1)} %param.16, f32[256,512]{1,0:T(8,128)S(1)} %fusion.29, bf16[256,1024]{1,0:T(8,128)(2,1)S(1)} %all_gather.3, f32[1024]{0:T(1024)S(1)} %copy-done.11, f32[256]{0:T(256)S(1)} %add_rsqrt_fusion), kind=kOutput, calls=%fused_computation.7 | convolution fusion | flops 538968064 | bytes 3675136 | tf_op jit(solution)/shard_map/dot_general | solution.py:26
  77.3 1.2 fusion.1
  78.5 0.7 convert_multiply_fusion.7
  79.2 1.3 select_reduce_fusion
  80.5 18.2 %reduce-scatter.2.cloned.1.call-done = bf16[256,256]{1,0:T(8,128)(2,1)} async-done(((bf16[256,1024]{1,0:T(8,128)(2,1)}), bf16[256,256]{1,0:T(8,128)(2,1)}) %reduce-scatter.2.cloned.1.call-update) | async-done | bytes 131088 | tf_op jit(solution)/shard_map/reduce_scatter | solution.py:445
  98.7 1.3 convolution_convert_fusion.1
  100.0 1.6 copy-done.2
  101.6 1.6 copy-done.3
  103.2 49.6 %shard_map.122 = bf16[8,128,256]{2,1,0:T(8,128)(2,1)S(1)} custom-call(bf16[8,128,256]{2,1,0:T(8,128)(2,1)S(1)} %bitcast.62, f32[1,1024]{1,0:T(1,128)S(1)} %bitcast.63, bf16[1,1024,1024]{2,1,0:T(8,128)(2,1)S(1)} %copy-done.1, bf16[1,1024,1024]{2,1,0:T(8,128)(2,1)S(1)} %copy-done.2, bf16[1,1024,1024]{2,1,0:T(8,128)(2,1)S(1)} %copy-done.3), custom_call_target="tpu_custom_call" | custom-call | flops 6442450944 | bytes 6291456 | tf_op jit(solution)/shard_map/pallas_call | solution.py:371
  152.8 1.0 fusion.3
  (41 shorter events, 2.0 us)
Async XLA Ops:
  6.5 67.0 %copy-start = (bf16[512,1024]{1,0:T(8,128)(2,1)S(1)}, bf16[512,1024]{1,0:T(8,128)(2,1)}, u32[]{:S(2)}) copy-start(bf16[512,1024]{1,0:T(8,128)(2,1)} %param.17) | copy-start | bytes 3145732
  6.5 92.1 %reduce-scatter.2.cloned.1.call-start = ((), (), s32[]{:S(2)}) async-start(), calls=%async_computation.1 | async-start | bytes 655360 | tf_op jit(solution)/shard_map/reduce_scatter | solution.py:445
  31.2 4.8 %copy-start.10 = (bf16[2,256,1,256]{3,1,2,0:T(8,128)(2,1)S(1)}, bf16[2,256,1,256]{3,1,2,0:T(8,128)(2,1)}, u32[]{:S(2)}) copy-start(bf16[2,256,1,256]{3,1,2,0:T(8,128)(2,1)} %param.13) | copy-start | bytes 786436
  42.0 23.4 %copy-start.7 = (bf16[256,256]{1,0:T(8,128)(2,1)S(1)}, bf16[256,256]{1,0:T(8,128)(2,1)}, u32[]{:S(2)}) copy-start(bf16[256,256]{1,0:T(8,128)(2,1)} %param.12) | copy-start | bytes 393220
  54.1 19.0 %copy-start.9 = (bf16[1024,512]{1,0:T(8,128)(2,1)S(1)}, bf16[1024,512]{1,0:T(8,128)(2,1)}, u32[]{:S(2)}) copy-start(bf16[1024,512]{1,0:T(8,128)(2,1)} %param.15) | copy-start | bytes 3145732
  54.1 19.0 %copy-start.11 = (f32[1024]{0:T(1024)S(1)}, f32[1024]{0:T(1024)}, u32[]{:S(2)}) copy-start(f32[1024]{0:T(1024)} %param.14) | copy-start | bytes 12292
  73.5 3.0 %copy-start.8 = (s32[256,2]{0,1:T(2,128)S(1)}, s32[256,2]{0,1:T(2,128)}, u32[]{:S(2)}) copy-start(s32[256,2]{0,1:T(2,128)} %param.22) | copy-start | bytes 6148
  76.5 23.5 %copy-start.1 = (bf16[1,1024,1024]{2,1,0:T(8,128)(2,1)S(1)}, bf16[1,1024,1024]{2,1,0:T(8,128)(2,1)}, u32[]{:S(2)}) copy-start(bf16[1,1024,1024]{2,1,0:T(8,128)(2,1)} %gate_hbm.1) | copy-start | bytes 6291460
  76.5 23.5 %copy-start.4 = (f32[1024]{0:T(1024)S(1)}, f32[1024]{0:T(1024)}, u32[]{:S(2)}) copy-start(f32[1024]{0:T(1024)} %param.18) | copy-start | bytes 12292
  100.0 1.6 copy-start.2
  101.6 1.6 copy-start.3
  103.2 49.6 %copy-start.5 = (bf16[1024,256]{1,0:T(8,128)(2,1)S(1)}, bf16[1024,256]{1,0:T(8,128)(2,1)}, u32[]{:S(2)}) copy-start(bf16[1024,256]{1,0:T(8,128)(2,1)} %select_reduce_fusion) | copy-start | bytes 1572868
  103.2 49.6 %copy-start.6 = (bf16[256,256]{1,0:T(8,128)(2,1)S(1)}, bf16[256,256]{1,0:T(8,128)(2,1)}, u32[]{:S(2)}) copy-start(bf16[256,256]{1,0:T(8,128)(2,1)} %reduce-scatter.2.cloned.1.call-done) | copy-start | bytes 393220
Sparse Core Ops, SparseCore 0:
  76.6 21.9 reduce-scatter.1

commit v4 on v2

--- a/solution.py
+++ b/solution.py
@@ -376,6 +376,263 @@
     return lax.all_to_all(expert_out, "freq", split_axis=0, concat_axis=0, tiled=True)
 
 
+def encode_kernel(
+    slabs,
+    src_ref,
+    filter_ref,
+    cos_ref,
+    sin_ref,
+    twist_ref,
+    undo_ref,
+    gain_ref,
+    gate_hbm,
+    up_hbm,
+    down_hbm,
+    out_ref,
+    gate_ref,
+    up_ref,
+    down_ref,
+    land1,
+    pack2,
+    land2,
+    cols_ref,
+    pack3,
+    land3,
+    pack4,
+    land4,
+    mixed_ref,
+    rows_ref,
+    normed_ref,
+    part_ref,
+    pair_ref,
+    turn_ref,
+    cross_ref,
+    weight_sem,
+    swap_send,
+    swap_recv,
+    side_send,
+    side_recv,
+):
+    me = lax.axis_index("freq")
+    chan = lax.axis_index("chan")
+    core = lax.axis_index("expert")
+    mine = chan * 2 + core
+    other = (1 - chan) * 2 + core
+    block, width = src_ref.shape[1], src_ref.shape[2]
+    length = slabs * block
+    half = jnp.bfloat16
+    loads = [
+        pltpu.make_async_copy(source, target, weight_sem.at[number])
+        for number, (source, target) in enumerate(
+            ((gate_hbm, gate_ref), (up_hbm, up_ref), (down_hbm, down_ref))
+        )
+    ]
+    for load in loads:
+        load.start()
+    barrier = pltpu.get_barrier_semaphore()
+    for k in range(1, slabs):
+        pl.semaphore_signal(
+            barrier, inc=1, device_id={"freq": lax.rem(me + k, slabs)}, device_id_type=pl.DeviceIdType.MESH
+        )
+    pl.semaphore_signal(barrier, inc=1, device_id={"chan": 1 - chan}, device_id_type=pl.DeviceIdType.MESH)
+    pl.semaphore_signal(barrier, inc=1, device_id={"expert": 1 - core}, device_id_type=pl.DeviceIdType.MESH)
+    pl.semaphore_wait(barrier, slabs + 1)
+    sent = []
+
+    def remote(source, target, send, recv, device):
+        copy = pltpu.make_async_remote_copy(
+            src_ref=source,
+            dst_ref=target,
+            send_sem=send,
+            recv_sem=recv,
+            device_id=device,
+            device_id_type=pl.DeviceIdType.MESH,
+        )
+        copy.start()
+        sent.append(copy)
+        return copy
+
+    def swap(number, source, land):
+        copies = []
+        for k in range(1, slabs):
+            peer = lax.rem(me + k, slabs)
+            copies.append(
+                remote(
+                    source.at[peer],
+                    land.at[k],
+                    swap_send.at[number, k],
+                    swap_recv.at[number, k],
+                    {"freq": peer},
+                )
+            )
+        land[0] = source[me]
+        for copy in copies:
+            copy.wait_recv()
+
+    def side(number, source, target, device):
+        return remote(source, target, side_send.at[number], side_recv.at[number], device)
+
+    def slot(source):
+        return lax.rem(me - source + slabs, slabs)
+
+    def turn_of(number):
+        angle = 2.0 * math.pi * (number % slabs) / slabs
+        return math.cos(angle), math.sin(angle)
+
+    def span(s):
+        return slice(s * block, (s + 1) * block)
+
+    swap(0, src_ref, land1)
+    signal = [land1[slot(s)].astype(jnp.float32) for s in range(slabs)]
+    for k in range(slabs):
+        re = sum(signal[s] * turn_of(s * k)[0] for s in range(slabs))
+        im = -sum(signal[s] * turn_of(s * k)[1] for s in range(slabs))
+        cos, sin = twist_ref[0, k], twist_ref[1, k]
+        pack2[k, :block] = (re * cos + im * sin).astype(half)
+        pack2[k, block:] = (im * cos - re * sin).astype(half)
+    swap(1, pack2, land2)
+    for s in range(slabs):
+        cols_ref[0, span(s)] = land2[slot(s), :block]
+        cols_ref[1, span(s)] = land2[slot(s), block:]
+    cos_long, sin_long = cos_ref[...], sin_ref[...]
+    col_re, col_im = cols_ref[0], cols_ref[1]
+    freq_re = matmul(cos_long, col_re) + matmul(sin_long, col_im)
+    freq_im = matmul(cos_long, col_im) - matmul(sin_long, col_re)
+    coef_re, coef_im = filter_ref[0].astype(jnp.float32), filter_ref[1].astype(jnp.float32)
+    shaped_re = (coef_re * freq_re - coef_im * freq_im).astype(half)
+    shaped_im = (coef_re * freq_im + coef_im * freq_re).astype(half)
+    back_re = matmul(cos_long, shaped_re) - matmul(sin_long, shaped_im)
+    back_im = matmul(cos_long, shaped_im) + matmul(sin_long, shaped_re)
+    spun_re = (back_re * undo_ref[0] - back_im * undo_ref[1]).astype(half)
+    spun_im = (back_im * undo_ref[0] + back_re * undo_ref[1]).astype(half)
+    for s in range(slabs):
+        pack3[s, :block] = spun_re[span(s)]
+        pack3[s, block:] = spun_im[span(s)]
+    swap(2, pack3, land3)
+    real = [land3[slot(k), :block].astype(jnp.float32) for k in range(slabs)]
+    imag = [land3[slot(k), block:].astype(jnp.float32) for k in range(slabs)]
+    for s in range(slabs):
+        pack4[s] = sum(
+            real[k] * turn_of(s * k)[0] - imag[k] * turn_of(s * k)[1] for k in range(slabs)
+        ).astype(half)
+    swap(3, pack4, land4)
+    for s in range(slabs):
+        mixed = src_ref[s].astype(jnp.float32) + land4[slot(s)].astype(jnp.float32) / (length * slabs)
+        mixed_ref[span(s)] = mixed
+        rows_ref[mine, span(s)] = mixed.astype(half)
+
+    to_cross = side(0, rows_ref.at[mine], rows_ref.at[mine], {"chan": 1 - chan})
+    to_sibling = side(1, rows_ref.at[mine], rows_ref.at[mine], {"expert": 1 - core})
+    to_cross.wait_recv()
+    forward = side(2, rows_ref.at[other], rows_ref.at[other], {"expert": 1 - core})
+    to_sibling.wait_recv()
+    forward.wait_recv()
+    quarters = [rows_ref[q].astype(jnp.float32) for q in range(4)]
+    total = sum(jnp.sum(x * x, axis=-1, keepdims=True) for x in quarters)
+    scale = lax.rsqrt(total / (4 * width) + EPS)
+    for q in range(4):
+        cols = slice(q * width, (q + 1) * width)
+        normed_ref[:, cols] = (quarters[q] * scale * gain_ref[:, cols]).astype(half)
+    for load in loads:
+        load.wait()
+    gate = matmul(normed_ref[...], gate_ref[...])
+    up = matmul(normed_ref[...], up_ref[...])
+    hidden = (gate / (1.0 + jnp.exp(-gate)) * up).astype(half)
+    for q in range(4):
+        part_ref[q] = matmul(hidden, down_ref[:, q * width : (q + 1) * width]).astype(half)
+    pairs = [
+        side(3 + c, part_ref.at[c * 2 + 1 - core], pair_ref.at[c], {"expert": 1 - core}) for c in range(2)
+    ]
+    for copy in pairs:
+        copy.wait_recv()
+
+    def both(q, c):
+        return part_ref[q].astype(jnp.float32) + pair_ref[c].astype(jnp.float32)
+
+    turn_ref[...] = both(other, 1 - chan).astype(half)
+    cross = side(5, turn_ref, cross_ref, {"chan": 1 - chan})
+    near = mixed_ref[...] + both(mine, chan)
+    cross.wait_recv()
+    out_ref[...] = near + cross_ref[...].astype(jnp.float32)
+    for copy in sent:
+        copy.wait_send()
+
+
+def encode_direct(spectra, filter_pair, gain, gate_w, up_w, down_w):
+    slabs = lax.axis_size("freq")
+    my_slab = lax.axis_index("freq")
+    length, width = spectra.shape
+    block = length // slabs
+    half = jnp.bfloat16
+    cos_long, sin_long = tables(length, length, length, 0)
+    twist = jnp.stack(tables(slabs, block, length * slabs, my_slab * block))[..., None]
+    undo = jnp.stack(tables(length, 1, length * slabs, my_slab))
+    dma = pltpu.SemaphoreType.DMA
+    vmem = pl.BlockSpec(memory_space=pltpu.VMEM)
+    hbm = pl.BlockSpec(memory_space=pl.ANY)
+    one, two = (slabs, block, width), (slabs, 2 * block, width)
+    return pl.pallas_call(
+        functools.partial(encode_kernel, slabs),
+        out_shape=jax.ShapeDtypeStruct((length, width), jnp.float32),
+        in_specs=[vmem] * 7 + [hbm] * 3,
+        out_specs=vmem,
+        scratch_shapes=[
+            pltpu.VMEM(gate_w.shape, half),
+            pltpu.VMEM(up_w.shape, half),
+            pltpu.VMEM(down_w.shape, half),
+            pltpu.VMEM(one, half),
+            pltpu.VMEM(two, half),
+            pltpu.VMEM(two, half),
+            pltpu.VMEM((2, length, width), half),
+            pltpu.VMEM(two, half),
+            pltpu.VMEM(two, half),
+            pltpu.VMEM(one, half),
+            pltpu.VMEM(one, half),
+            pltpu.VMEM((length, width), jnp.float32),
+            pltpu.VMEM((4, length, width), half),
+            pltpu.VMEM((length, 4 * width), half),
+            pltpu.VMEM((4, length, width), half),
+            pltpu.VMEM((2, length, width), half),
+            pltpu.VMEM((length, width), half),
+            pltpu.VMEM((length, width), half),
+            dma((3,)),
+            dma((4, slabs)),
+            dma((4, slabs)),
+            dma((6,)),
+            dma((6,)),
+        ],
+        compiler_params=pltpu.CompilerParams(
+            collective_id=2, has_side_effects=True, vmem_limit_bytes=28 * 1024 * 1024
+        ),
+    )(
+        spectra.reshape(one),
+        filter_pair[:, :, 0],
+        cos_long.astype(half),
+        sin_long.astype(half),
+        twist,
+        undo,
+        gain[None],
+        gate_w,
+        up_w,
+        down_w,
+    )
+
+
+def encode_plain(spectra, spectral_filter, norm_gain, mlp_gate, mlp_up, mlp_down):
+    signal = spectra.astype(jnp.float32)
+    mixed_sum = signal + spectral_mix(signal, spectral_filter)
+    full_rows = lax.all_gather(
+        mixed_sum.astype(jnp.bfloat16), ("chan", "expert"), axis=1, tiled=True
+    )
+    hidden = gated(rms_rows(full_rows, norm_gain), mlp_gate, mlp_up)
+    return mixed_sum + lax.psum_scatter(
+        matmul(hidden, mlp_down).astype(jnp.bfloat16),
+        ("chan", "expert"),
+        scatter_dimension=1,
+        tiled=True,
+    ).astype(jnp.float32)
+
+
 def body(
     spectra,
     spectral_filter,
@@ -390,18 +647,9 @@
     routes,
     combine,
 ):
-    signal = spectra.astype(jnp.float32)
-    mixed_sum = signal + spectral_mix(signal, spectral_filter)
-    full_rows = lax.all_gather(
-        mixed_sum.astype(jnp.bfloat16), ("chan", "expert"), axis=1, tiled=True
-    )
-    hidden = gated(rms_rows(full_rows, norm_gain), mlp_gate, mlp_up)
-    encoded = mixed_sum + lax.psum_scatter(
-        matmul(hidden, mlp_down).astype(jnp.bfloat16),
-        ("chan", "expert"),
-        scatter_dimension=1,
-        tiled=True,
-    ).astype(jnp.float32)
+    by_four = lax.axis_size("chan") == 2 and lax.axis_size("expert") == 2
+    encode = encode_direct if by_four and spectra.shape[0] % (16 * lax.axis_size("freq")) == 0 else encode_plain
+    encoded = encode(spectra, spectral_filter, norm_gain, mlp_gate, mlp_up, mlp_down)
     encoded_half = encoded.astype(jnp.bfloat16)
     slabs = lax.axis_size("freq")
     length = spectra.shape[0]

time: 161 us -> 103 us (0.64)
  Pallas kernels: 49.8 us -> 90.3 us
  waiting for transfers between devices: 30.3 us -> 0 us
  blocking collectives: 28.7 us -> 0 us
  matrix products: 16.8 us -> 1.59 us
  between operations: 13.7 us -> 0.15 us
  starting transfers between devices: 10.9 us -> 0 us
    pallas_call x0 -> x1, Pallas kernels: none -> 41.9 us  [encode_direct(): pl.pallas_call(functools.partial(encode_kernel, slabs), out_shape=jax.Sha...]
    all_to_all x2 -> x0, blocking collectives: 21.2 us -> none  [across_slabs(): lax.all_to_all(values.astype(jnp.bfloat16), 'freq', split_axis=0, concat_...]
    all_to_all x2 -> x0, waiting for transfers between devices: 15.2 us -> none  [across_slabs(): lax.all_to_all(values.astype(jnp.bfloat16), 'freq', split_axis=0, concat_...]
    dot_general x16 -> x2, matrix products: 15.8 us -> 0.59 us  [matmul(): return jnp.dot(left, right, preferred_element_type=jnp.float32)]
    reduce_scatter x1 -> x0, waiting for transfers between devices: 15 us -> none  [body(): lax.psum_scatter(matmul(hidden, mlp_down).astype(jnp.bfloat16), ('chan',...]
    all_to_all x2 -> x0, starting transfers between devices: 10.8 us -> none  [across_slabs(): lax.all_to_all(values.astype(jnp.bfloat16), 'freq', split_axis=0, concat_...]
    all_gather x1 -> x0, blocking collectives: 7.48 us -> none  [body(): lax.all_gather(mixed_sum.astype(jnp.bfloat16), ('chan', 'expert'), axis=1...]
    unnamed x29 -> x21, local copies, waits for them, and re-layouts: 3.52 us -> 6.45 us
  transfers between devices with their start and end apart: 3 -> 0, of which waited for: 3 -> 0; matrix products, arithmetic and copies ran while one was open for 3% -> 0% of each run, Pallas kernels for 0% -> 0%
where the time goes in v4:
time: 103 us
  Pallas kernels  90.3 us (88%)
  local copies, waits for them, and re-layouts  7.13 us (7%)
  other arithmetic  3.54 us (3%)
  matrix products  1.59 us (2%)
    pallas_call x1, Pallas kernels, experts_direct(): pl.pallas_call(functools.partial(experts_kernel, slabs, per), out_shape=j...  48.4 us
    pallas_call x1, Pallas kernels, encode_direct(): pl.pallas_call(functools.partial(encode_kernel, slabs), out_shape=jax.Sha...  41.9 us
    unnamed x21, local copies, waits for them, and re-layouts  6.45 us

profile of v4, /device:TPU:0, one launch (start us, length us, event | category | flops | bytes accessed | tf_op | source)
XLA Modules:
  0.0 102.7 jit_solution(6875418889846114674)
XLA Ops:
  0.0 0.0 copy-start.3
  0.0 0.1 fusion.24
  0.1 0.8 convert_multiply_fusion
  0.9 0.1 fusion.20
  0.9 0.8 copy.34
  1.7 0.1 eq.36
  1.9 0.3 fusion.3
  2.2 0.1 reduce_sum.21
  2.3 0.1 copy.35
  2.4 0.7 multiply_add_fusion
  3.1 0.2 copy.32.twist_ref
  3.3 0.1 copy.33.undo_ref
  3.4 0.4 fusion
  3.8 1.1 %sine_convert_fusion = (bf16[256,256]{1,0:T(8,128)(2,1)S(1)}, bf16[256,256]{1,0:T(8,128)(2,1)S(1)}) fusion(), kind=kLoop, calls=%fused_computation.17 | loop fusion | flops 1048576 | bytes 262144 | tf_op jit(solution)/shard_map/convert_element_type | solution.py:611
  4.9 0.0 copy-done
  4.9 0.0 copy-done.3
  4.9 0.0 copy-start.1
  4.9 1.2 %copy-done.1 = bf16[1024,512]{1,0:T(8,128)(2,1)S(1)} copy-done((bf16[1024,512]{1,0:T(8,128)(2,1)S(1)}, bf16[1024,512]{1,0:T(8,128)(2,1)}, u32[]{:S(2)}) %copy-start.1) | copy-done | bytes 1048600
  6.2 0.0 copy-start.2
  6.2 1.2 %copy-done.2 = bf16[512,1024]{1,0:T(8,128)(2,1)S(1)} copy-done((bf16[512,1024]{1,0:T(8,128)(2,1)S(1)}, bf16[512,1024]{1,0:T(8,128)(2,1)}, u32[]{:S(2)}) %copy-start.2) | copy-done | bytes 1048600
  7.4 0.9 copy-done.4
  8.3 0.7 copy-done.5
  9.0 41.9 %shard_map.118 = f32[256,256]{1,0:T(8,128)S(1)} custom-call(bf16[8,32,256]{2,1,0:T(8,128)(2,1)S(1)} %bitcast.14, bf16[2,256,256]{2,1,0:T(8,128)(2,1)S(1)} %bitcast.13, bf16[256,256]{1,0:T(8,128)(2,1)S(1)} %get-tuple-element.10.cos_ref, bf16[256,256]{1,0:T(8,128)(2,1)S(1)} %get-tuple-element.9.sin_ref, f32[2,8,32,1]{3,2,1,0:T(8,128)S(1)} %copy.32.twist_ref, ...), custom_call_target="tpu_custom_call" | custom-call | tf_op jit(solution)/shard_map/pallas_call | solution.py:574
  50.9 0.3 convolution_convert_fusion
  51.2 0.0 copy-done.6
  51.2 0.0 copy-done.7
  51.2 0.0 copy-done.9
  51.2 0.0 copy-start.8
  51.2 1.6 %copy-done.8 = bf16[1,1024,1024]{2,1,0:T(8,128)(2,1)S(1)} copy-done((bf16[1,1024,1024]{2,1,0:T(8,128)(2,1)S(1)}, bf16[1,1024,1024]{2,1,0:T(8,128)(2,1)}, u32[]{:S(2)}) %copy-start.8) | copy-done | bytes 2097176
  52.8 48.4 %shard_map.119 = bf16[8,128,256]{2,1,0:T(8,128)(2,1)S(1)} custom-call(bf16[8,128,256]{2,1,0:T(8,128)(2,1)S(1)} %bitcast.11, f32[1,1024]{1,0:T(1,128)S(1)} %bitcast.16, bf16[1,1024,1024]{2,1,0:T(8,128)(2,1)S(1)} %copy-done.6, bf16[1,1024,1024]{2,1,0:T(8,128)(2,1)S(1)} %copy-done.7, bf16[1,1024,1024]{2,1,0:T(8,128)(2,1)S(1)} %copy-done.8), custom_call_target="tpu_custom_call" | custom-call | flops 6442450944 | bytes 6291456 | tf_op jit(solution)/shard_map/pallas_call | solution.py:325
  101.3 0.5 select_reduce_fusion
  101.7 1.0 fusion.1
  (9 shorter events, 0.0 us)
Async XLA Ops:
  0.0 4.9 %copy-start = (bf16[1024,512]{1,0:T(8,128)(2,1)S(1)}, bf16[1024,512]{1,0:T(8,128)(2,1)}, u32[]{:S(2)}) copy-start(bf16[1024,512]{1,0:T(8,128)(2,1)} %gate_hbm.2) | copy-start | bytes 3145732
  0.0 4.9 %copy-start.3 = (bf16[2,256,1,256]{3,1,2,0:T(8,128)(2,1)S(1)}, bf16[2,256,1,256]{3,1,2,0:T(8,128)(2,1)}, u32[]{:S(2)}) copy-start(bf16[2,256,1,256]{3,1,2,0:T(8,128)(2,1)} %param.13) | copy-start | bytes 786436
  4.9 1.2 %copy-start.1 = (bf16[1024,512]{1,0:T(8,128)(2,1)S(1)}, bf16[1024,512]{1,0:T(8,128)(2,1)}, u32[]{:S(2)}) copy-start(bf16[1024,512]{1,0:T(8,128)(2,1)} %up_hbm.2) | copy-start | bytes 3145732
  6.2 1.2 %copy-start.2 = (bf16[512,1024]{1,0:T(8,128)(2,1)S(1)}, bf16[512,1024]{1,0:T(8,128)(2,1)}, u32[]{:S(2)}) copy-start(bf16[512,1024]{1,0:T(8,128)(2,1)} %down_hbm.2) | copy-start | bytes 3145732
  7.4 0.9 copy-start.4
  8.3 0.7 copy-start.5
  9.0 42.2 %copy-start.6 = (bf16[1,1024,1024]{2,1,0:T(8,128)(2,1)S(1)}, bf16[1,1024,1024]{2,1,0:T(8,128)(2,1)}, u32[]{:S(2)}) copy-start(bf16[1,1024,1024]{2,1,0:T(8,128)(2,1)} %gate_hbm.3) | copy-start | bytes 6291460
  9.0 42.2 %copy-start.7 = (bf16[1,1024,1024]{2,1,0:T(8,128)(2,1)S(1)}, bf16[1,1024,1024]{2,1,0:T(8,128)(2,1)}, u32[]{:S(2)}) copy-start(bf16[1,1024,1024]{2,1,0:T(8,128)(2,1)} %up_hbm.3) | copy-start | bytes 6291460
  9.0 42.3 %copy-start.9 = (f32[1024]{0:T(1024)S(1)}, f32[1024]{0:T(1024)}, u32[]{:S(2)}) copy-start(f32[1024]{0:T(1024)} %param.18) | copy-start | bytes 12292
  51.2 1.6 %copy-start.8 = (bf16[1,1024,1024]{2,1,0:T(8,128)(2,1)S(1)}, bf16[1,1024,1024]{2,1,0:T(8,128)(2,1)}, u32[]{:S(2)}) copy-start(bf16[1,1024,1024]{2,1,0:T(8,128)(2,1)} %down_hbm.3) | copy-start | bytes 6291460

commit v5 on v4

--- a/solution.py
+++ b/solution.py
@@ -3,6 +3,7 @@
 
 import jax
 import jax.numpy as jnp
+import numpy as np
 from jax import lax
 from jax.experimental import pallas as pl
 from jax.experimental.pallas import tpu as pltpu
@@ -138,15 +139,6 @@
     for load in loads:
         load.start()
 
-    barrier = pltpu.get_barrier_semaphore()
-    for k in range(1, slabs):
-        pl.semaphore_signal(
-            barrier, inc=1, device_id={"freq": lax.rem(me + k, slabs)}, device_id_type=pl.DeviceIdType.MESH
-        )
-    pl.semaphore_signal(barrier, inc=1, device_id={"chan": 1 - chan}, device_id_type=pl.DeviceIdType.MESH)
-    pl.semaphore_signal(barrier, inc=1, device_id={"expert": 1 - core}, device_id_type=pl.DeviceIdType.MESH)
-    pl.semaphore_wait(barrier, slabs + 1)
-
     def remote(source, target, send, recv, device):
         return pltpu.make_async_remote_copy(
             src_ref=source,
@@ -311,58 +303,6 @@
         pair(0, i).wait_send()
         pair(1, i).wait_send()
         cross(i).wait_send()
-
-
-def experts_direct(outgoing, gain, gate_w, up_w, down_w):
-    slabs, capacity, width = outgoing.shape
-    per = max(1, 256 // capacity)
-    groups = slabs // per
-    hidden = gate_w.shape[2]
-    half = jnp.bfloat16
-    dma = pltpu.SemaphoreType.DMA
-    vmem = pl.BlockSpec(memory_space=pltpu.VMEM)
-    hbm = pl.BlockSpec(memory_space=pl.ANY)
-    return pl.pallas_call(
-        functools.partial(experts_kernel, slabs, per),
-        out_shape=jax.ShapeDtypeStruct(outgoing.shape, half),
-        in_specs=[vmem, vmem, hbm, hbm, hbm],
-        out_specs=vmem,
-        scratch_shapes=[
-            pltpu.VMEM(gate_w.shape, half),
-            pltpu.VMEM(up_w.shape, half),
-            pltpu.VMEM(down_w.shape, half),
-            pltpu.VMEM((4, slabs, capacity, width), half),
-            pltpu.VMEM((per * capacity, 4 * width), half),
-            pltpu.VMEM((per * capacity, hidden), half),
-            pltpu.VMEM((4, slabs, capacity, width), half),
-            pltpu.VMEM((2, slabs, capacity, width), half),
-            pltpu.VMEM((slabs, capacity, width), half),
-            pltpu.VMEM((slabs, capacity, width), half),
-            pltpu.VMEM((slabs, capacity, width), half),
-            pltpu.VMEM((slabs, capacity, width), half),
-            dma((3,)),
-            dma((slabs,)),
-            dma((slabs,)),
-            dma((groups,)),
-            dma((groups,)),
-            dma((groups,)),
-            dma((groups,)),
-            dma((groups,)),
-            dma((groups,)),
-            dma((2, groups)),
-            dma((2, groups)),
-            dma((groups,)),
-            dma((groups,)),
-            dma((slabs,)),
-            dma((slabs,)),
-        ],
-        compiler_params=pltpu.CompilerParams(
-            collective_id=1, has_side_effects=True, vmem_limit_bytes=36 * 1024 * 1024
-        ),
-        cost_estimate=pl.CostEstimate(
-            flops=6 * slabs * capacity * 4 * width * hidden, bytes_accessed=3 * 8 * width * hidden, transcendentals=0
-        ),
-    )(outgoing, gain[None], gate_w, up_w, down_w)
 
 
 def experts_plain(outgoing, gain, gate_w, up_w, down_w):
@@ -558,25 +498,36 @@
         copy.wait_send()
 
 
-def encode_direct(spectra, filter_pair, gain, gate_w, up_w, down_w):
+def layer_kernel(slabs, per, split, *refs):
+    encode_in, (table_ref, gain_ref), weights = refs[:10], refs[10:12], refs[12:15]
+    (encoded_ref, back_ref), scratch = refs[15:17], refs[17:]
+    encode_kernel(slabs, *encode_in, encoded_ref, *scratch[:split])
+    outgoing_ref = scratch[split]
+    half = encoded_ref[...].astype(jnp.bfloat16)
+    for k in range(slabs):
+        outgoing_ref[k] = matmul(table_ref[k], half).astype(jnp.bfloat16)
+    experts_kernel(slabs, per, outgoing_ref, gain_ref, *weights, back_ref, *scratch[split + 1 :])
+
+
+def layer_direct(spectra, filter_pair, gain, gate_w, up_w, down_w, send_table, egain, egate, eup, edown):
     slabs = lax.axis_size("freq")
     my_slab = lax.axis_index("freq")
     length, width = spectra.shape
+    capacity = send_table.shape[0] // slabs
+    per = max(1, 256 // capacity)
+    groups = slabs // per
+    hidden = egate.shape[2]
     block = length // slabs
     half = jnp.bfloat16
-    cos_long, sin_long = tables(length, length, length, 0)
+    steps = np.arange(length)
+    angle = (steps[:, None] * steps[None, :] % length) * (2.0 * math.pi / length)
     twist = jnp.stack(tables(slabs, block, length * slabs, my_slab * block))[..., None]
     undo = jnp.stack(tables(length, 1, length * slabs, my_slab))
     dma = pltpu.SemaphoreType.DMA
     vmem = pl.BlockSpec(memory_space=pltpu.VMEM)
     hbm = pl.BlockSpec(memory_space=pl.ANY)
     one, two = (slabs, block, width), (slabs, 2 * block, width)
-    return pl.pallas_call(
-        functools.partial(encode_kernel, slabs),
-        out_shape=jax.ShapeDtypeStruct((length, width), jnp.float32),
-        in_specs=[vmem] * 7 + [hbm] * 3,
-        out_specs=vmem,
-        scratch_shapes=[
+    encode_scratch = [
             pltpu.VMEM(gate_w.shape, half),
             pltpu.VMEM(up_w.shape, half),
             pltpu.VMEM(down_w.shape, half),
@@ -600,21 +551,62 @@
             dma((4, slabs)),
             dma((6,)),
             dma((6,)),
-        ],
+        ]
+    expert_scratch = [
+            pltpu.VMEM(egate.shape, half),
+            pltpu.VMEM(eup.shape, half),
+            pltpu.VMEM(edown.shape, half),
+            pltpu.VMEM((4, slabs, capacity, width), half),
+            pltpu.VMEM((per * capacity, 4 * width), half),
+            pltpu.VMEM((per * capacity, hidden), half),
+            pltpu.VMEM((4, slabs, capacity, width), half),
+            pltpu.VMEM((2, slabs, capacity, width), half),
+            pltpu.VMEM((slabs, capacity, width), half),
+            pltpu.VMEM((slabs, capacity, width), half),
+            pltpu.VMEM((slabs, capacity, width), half),
+            pltpu.VMEM((slabs, capacity, width), half),
+            dma((3,)),
+            dma((slabs,)),
+            dma((slabs,)),
+            dma((groups,)),
+            dma((groups,)),
+            dma((groups,)),
+            dma((groups,)),
+            dma((groups,)),
+            dma((groups,)),
+            dma((2, groups)),
+            dma((2, groups)),
+            dma((groups,)),
+            dma((groups,)),
+            dma((slabs,)),
+            dma((slabs,)),
+        ]
+    slots = (slabs, capacity, width)
+    return pl.pallas_call(
+        functools.partial(layer_kernel, slabs, per, len(encode_scratch)),
+        out_shape=(jax.ShapeDtypeStruct((length, width), jnp.float32), jax.ShapeDtypeStruct(slots, half)),
+        in_specs=[vmem] * 7 + [hbm] * 3 + [vmem] * 2 + [hbm] * 3,
+        out_specs=(vmem, vmem),
+        scratch_shapes=encode_scratch + [pltpu.VMEM(slots, half)] + expert_scratch,
         compiler_params=pltpu.CompilerParams(
-            collective_id=2, has_side_effects=True, vmem_limit_bytes=28 * 1024 * 1024
+            collective_id=2, has_side_effects=True, vmem_limit_bytes=48 * 1024 * 1024
         ),
     )(
         spectra.reshape(one),
         filter_pair[:, :, 0],
-        cos_long.astype(half),
-        sin_long.astype(half),
+        jnp.asarray(np.cos(angle), half),
+        jnp.asarray(np.sin(angle), half),
         twist,
         undo,
         gain[None],
         gate_w,
         up_w,
         down_w,
+        send_table.reshape(slabs, capacity, length),
+        egain[None],
+        egate,
+        eup,
+        edown,
     )
 
 
@@ -647,10 +639,6 @@
     routes,
     combine,
 ):
-    by_four = lax.axis_size("chan") == 2 and lax.axis_size("expert") == 2
-    encode = encode_direct if by_four and spectra.shape[0] % (16 * lax.axis_size("freq")) == 0 else encode_plain
-    encoded = encode(spectra, spectral_filter, norm_gain, mlp_gate, mlp_up, mlp_down)
-    encoded_half = encoded.astype(jnp.bfloat16)
     slabs = lax.axis_size("freq")
     length = spectra.shape[0]
     capacity = min(length, 4 * length // slabs)
@@ -667,16 +655,22 @@
     send_table = jnp.any(placed, axis=2).astype(jnp.bfloat16)
     shares = combine.astype(jnp.float32) / 8.0
     merge_table = jnp.sum(jnp.where(placed, shares[None], 0.0), axis=2).astype(jnp.bfloat16)
-    outgoing = matmul(send_table, encoded_half).astype(jnp.bfloat16)
-    outgoing = outgoing.reshape(slabs, capacity, -1)
+    encoder = (spectra, spectral_filter, norm_gain, mlp_gate, mlp_up, mlp_down)
+    experts = (expert_gain, expert_gate, expert_up, expert_down)
     direct = (
         lax.axis_size("chan") == 2
         and lax.axis_size("expert") == 2
+        and length % (16 * slabs) == 0
         and capacity % 16 == 0
         and slabs % max(1, 256 // capacity) == 0
     )
-    experts = experts_direct if direct else experts_plain
-    returned = experts(outgoing, expert_gain, expert_gate, expert_up, expert_down).reshape(slots_all, -1)
+    if direct:
+        encoded, returned = layer_direct(*encoder, send_table, *experts)
+    else:
+        encoded = encode_plain(*encoder)
+        outgoing = matmul(send_table, encoded.astype(jnp.bfloat16)).astype(jnp.bfloat16)
+        returned = experts_plain(outgoing.reshape(slabs, capacity, -1), *experts)
+    returned = returned.reshape(slots_all, -1)
     routed_sum = lax.dot_general(
         merge_table, returned, (((0,), (0,)), ((), ())), preferred_element_type=jnp.float32
     )

time: 103 us -> 97.1 us (0.943)
  Pallas kernels: 90.3 us -> 87.9 us
  other arithmetic: 3.54 us -> 1.78 us
  local copies, waits for them, and re-layouts: 7.13 us -> 5.67 us
    pallas_call x2 -> x1, Pallas kernels: 90.3 us -> 87.9 us  [layer_direct(): pl.pallas_call(functools.partial(layer_kernel, slabs, per, len(encode_scr...]
    unnamed x21, local copies, waits for them, and re-layouts: 6.45 us -> 4.99 us
where the time goes in v5:
time: 97.1 us; the launch traced here: 96.8 us
  Pallas kernels  87.9 us (91%)
  local copies, waits for them, and re-layouts  5.67 us (6%)
  other arithmetic  1.78 us (2%)
  matrix products  1.28 us (1%)
    pallas_call x1, Pallas kernels, layer_direct(): pl.pallas_call(functools.partial(layer_kernel, slabs, per, len(encode_scr...  87.9 us
    unnamed x21, local copies, waits for them, and re-layouts  4.99 us

profile of v5, /device:TPU:0, one launch (start us, length us, event | category | flops | bytes accessed | tf_op | source)
XLA Modules:
  0.0 96.8 jit_solution(11150099572202119818)
XLA Ops:
  0.0 0.0 copy-start.3
  0.0 0.0 copy-start.7
  0.0 0.0 copy-start.8
  0.0 0.0 copy-start
  0.0 0.0 copy-start.1
  0.0 0.1 fusion.13
  0.1 0.2 copy.36.refs_4_
  0.3 0.1 fusion.17
  0.4 0.1 copy.37.refs_5_
  0.5 1.0 %copy.34 = s32[256,2]{1,0:T(8,128)S(1)} copy(s32[256,2]{0,1:T(2,128)} %param.24) | data formatting | bytes 4096 | tf_op args[10]
  1.6 0.1 eq.34
  1.7 0.3 fusion.3
  2.0 0.1 reduce_sum.21
  2.1 0.1 copy.35
  2.2 0.7 multiply_add_fusion
  2.9 0.4 fusion
  3.3 0.1 convert_element_type.67
  3.4 0.0 copy-done.3
  3.4 0.0 copy-done.7
  3.4 0.0 copy-done.8
  3.4 0.0 copy-done
  3.4 0.0 copy-done.1
  3.4 0.0 copy-start.2
  3.5 1.2 %copy-done.2 = bf16[512,1024]{1,0:T(8,128)(2,1)S(1)} copy-done((bf16[512,1024]{1,0:T(8,128)(2,1)S(1)}, bf16[512,1024]{1,0:T(8,128)(2,1)}, u32[]{:S(2)}) %copy-start.2) | copy-done | bytes 1048600
  4.7 0.0 copy-start.4
  4.7 0.9 copy-done.4
  5.6 0.9 copy-done.5
  6.5 0.9 copy-done.6
  7.4 87.9 %shard_map.136 = (f32[256,256]{1,0:T(8,128)S(1)}, bf16[8,128,256]{2,1,0:T(8,128)(2,1)S(1)}) custom-call(bf16[8,32,256]{2,1,0:T(8,128)(2,1)S(1)} %bitcast.13, bf16[2,256,256]{2,1,0:T(8,128)(2,1)S(1)} %bitcast.12, bf16[256,256]{1,0:T(8,128)(2,1)S(1)} %copy-done.5, bf16[256,256]{1,0:T(8,128)(2,1)S(1)} %copy-done.6, f32[2,8,32,1]{3,2,1,0:T(8,128)S(1)} %copy.36.refs_4_, ...), custom_call_target="tpu_custom_call" | custom-call | tf_op jit(solution)/shard_map/pallas_call | solution.py:585
  95.3 0.0 copy-done.9
  95.3 0.5 select_reduce_fusion
  95.8 1.0 %fusion.1 = bf16[256,256]{1,0:T(8,128)(2,1)} fusion(f32[256,256]{1,0:T(8,128)S(1)} %get-tuple-element.7, bf16[1024,256]{1,0:T(8,128)(2,1)S(1)} %bitcast.11, bf16[1024,256]{1,0:T(8,128)(2,1)S(1)} %select_reduce_fusion), kind=kOutput, calls=%fused_computation.4 | convolution fusion | flops 134348800 | bytes 1441792 | tf_op jit(solution)/shard_map/dot_general | solution.py:674
  (7 shorter events, 0.0 us)
Async XLA Ops:
  0.0 3.4 %copy-start.3 = (bf16[2,256,1,256]{3,1,2,0:T(8,128)(2,1)S(1)}, bf16[2,256,1,256]{3,1,2,0:T(8,128)(2,1)}, u32[]{:S(2)}) copy-start(bf16[2,256,1,256]{3,1,2,0:T(8,128)(2,1)} %param.15) | copy-start | bytes 786436
  0.0 3.4 %copy-start.7 = (f32[1024]{0:T(1024)S(1)}, f32[1024]{0:T(1024)}, u32[]{:S(2)}) copy-start(f32[1024]{0:T(1024)} %param.16) | copy-start | bytes 12292
  0.0 3.4 %copy-start.8 = (f32[1024]{0:T(1024)S(1)}, f32[1024]{0:T(1024)}, u32[]{:S(2)}) copy-start(f32[1024]{0:T(1024)} %param.20) | copy-start | bytes 12292
  0.0 3.4 %copy-start = (bf16[1024,512]{1,0:T(8,128)(2,1)S(1)}, bf16[1024,512]{1,0:T(8,128)(2,1)}, u32[]{:S(2)}) copy-start(bf16[1024,512]{1,0:T(8,128)(2,1)} %refs_7_.1) | copy-start | bytes 3145732
  0.0 3.4 %copy-start.1 = (bf16[1024,512]{1,0:T(8,128)(2,1)S(1)}, bf16[1024,512]{1,0:T(8,128)(2,1)}, u32[]{:S(2)}) copy-start(bf16[1024,512]{1,0:T(8,128)(2,1)} %refs_8_.1) | copy-start | bytes 3145732
  3.4 1.2 %copy-start.2 = (bf16[512,1024]{1,0:T(8,128)(2,1)S(1)}, bf16[512,1024]{1,0:T(8,128)(2,1)}, u32[]{:S(2)}) copy-start(bf16[512,1024]{1,0:T(8,128)(2,1)} %refs_9_.1) | copy-start | bytes 3145732
  4.7 0.9 copy-start.4
  5.6 0.9 copy-start.5
  6.5 0.9 copy-start.6
  7.4 87.9 %copy-start.9 = (s32[256,2]{0,1:T(2,128)S(1)}, s32[256,2]{0,1:T(2,128)}, u32[]{:S(2)}) copy-start(s32[256,2]{0,1:T(2,128)} %param.25) | copy-start | bytes 6148
